TPU v7x, 512 devices: a whole 4x8x8 slice. The times are simulated.
512 devices in a mesh: node: 32 (over x, y), head: 16 (over z, core).
Axes of the slice: x: 4, y: 8, z: 8, core: 2. Of those that a mesh axis runs over, the one named last changes fastest.
Arguments:
- states: bfloat16 [256, 5376], P(None, 'node'), may hold values from -24 to 24
- w_query: bfloat16 [5376, 4096], P('node', 'head'), may hold values from -0.078125 to 0.078125
- w_key_value: bfloat16 [5376, 4096], P('node', 'head'), may hold values from -0.078125 to 0.078125
- w_out: bfloat16 [4096, 5376], P('head', 'node'), may hold values from -9 to 9
- post_gain: float32 [5376], P('node'), may hold values from 0.5 to 1.5
- cache: bfloat16 [3072, 64, 16, 256], P('node', None, 'head'), may hold values from -244 to 244
- tails: bfloat16 [256, 64, 16, 256], P('node', None, 'head'), may hold values from -6 to 6
- lengths: int32 [256], P('node'), may hold values from 0 to 63, as said below
- ancestry: int32 [256, 128], replicated, may hold values from 0 to 1, as said below
- block_node: int32 [3072], P('node'), may hold values from 0 to 127, as said below
- matching: int32 [1024], replicated, may hold values from 0 to 255, as said below
Outputs:
- branch: bfloat16 [256, 5376], P('head', 'node')
- children: bfloat16 [1024, 64, 16, 256], P('node', None, 'head')
Inputs may be any that keep to these rules, and one draw needn't show every extreme that they name: `lengths`: some leaf has 0 and some has 63. `ancestry`: row l marks the path from node 0, the shared prompt, to the node of leaf l, both ends included. `block_node`: node 0 is the shared prompt. `matching`: leaf l is homed on node index l // 8; the 32 children on one node index copy from leaves of exactly 32 node indices, exactly one child from each.
All inputs are finite; a program needn't handle non-finite values.
Results may differ from a plain program's by a relative error of at most 0.0095.
The roundings to bfloat16 on the way count: a program that leaves them out, or rounds other values in their place, can miss the bound.
Values may be sent and summed in bfloat16 or wider, within the bound.
No kernel may reach another device: no remote copies, remote signals or barrier semaphores. Data moves between devices by JAX's collectives and lax.ppermute only.
A program may use at most 64 MiB of HBM per device.

v0:
```python
import jax
import jax.numpy as jnp
from jax import lax
from jax.sharding import PartitionSpec as P

D = 5376
HEADS = 32
KVH = 16
HD = 128
BLK = 64


score_scale = 168.0 ** (-0.5)
neg_big = -1e30
epsilon = 1e-06


def shards(
    states,
    w_query,
    w_key_value,
    w_out,
    post_gain,
    cache,
    tails,
    lengths,
    ancestry,
    block_node,
    matching,
):
    node_count = lax.axis_size("node")
    node_index = lax.axis_index("node")
    leaves_all = states.shape[0]
    leaf_dev = leaves_all // node_count
    group_q = HEADS // KVH
    kv_dev = w_key_value.shape[1] // (2 * HD)
    query_cols = w_query.shape[1]
    projected = lax.psum_scatter(
        jnp.concatenate(
            [
                jnp.dot(states, w_query, preferred_element_type=jnp.float32),
                jnp.dot(states, w_key_value, preferred_element_type=jnp.float32),
            ],
            axis=1,
        ),
        "node",
        scatter_dimension=0,
        tiled=True,
    )
    query_mine = projected[:, :query_cols].astype(jnp.bfloat16)
    fresh_mine = projected[:, query_cols:].astype(jnp.bfloat16).reshape(leaf_dev, kv_dev, 2 * HD)
    queries = lax.all_gather(query_mine, "node", axis=0, tiled=True)
    rows_all = leaves_all * group_q
    head_query = (
        queries.reshape(leaves_all, kv_dev, group_q, HD)
        .transpose(1, 0, 2, 3)
        .reshape(kv_dev, rows_all, HD)
    )
    node_total = ancestry.shape[1]
    node_onehot = (block_node[:, None] == jnp.arange(node_total, dtype=jnp.int32)[None, :]).astype(
        jnp.float32
    )
    visible = (
        jnp.dot(ancestry.astype(jnp.float32), node_onehot.T, preferred_element_type=jnp.float32)
        > 0.5
    )
    local_blocks = cache.shape[0]
    group_blocks = 16
    group_total = local_blocks // group_blocks
    cache_groups = cache.reshape(group_total, group_blocks * BLK, kv_dev, 2 * HD)
    visible_groups = visible.reshape(leaves_all, group_total, group_blocks).transpose(1, 0, 2)

    def masked_scores(group_kv, group_visible):
        scores = (
            jnp.einsum(
                "hqd,khd->hqk", head_query, group_kv[..., :HD], preferred_element_type=jnp.float32
            )
            * score_scale
        )
        keep_mask = jnp.repeat(jnp.repeat(group_visible, BLK, axis=1), group_q, axis=0)[None]
        return (scores, keep_mask)

    def max_group(run_max, group_item):
        scores, keep_mask = masked_scores(group_item[0], group_item[1])
        return (jnp.maximum(run_max, jnp.max(jnp.where(keep_mask, scores, neg_big), axis=-1)), None)

    part_max, _ = lax.scan(
        max_group,
        jnp.full((kv_dev, rows_all), neg_big, jnp.float32),
        (cache_groups, visible_groups),
    )
    own_rows = leaf_dev * group_q
    own_start = node_index * own_rows
    own_query = query_mine.reshape(leaf_dev, kv_dev, group_q, HD)
    tail_scores = (
        jnp.einsum(
            "lhgd,lrhd->hlgr", own_query, tails[..., :HD], preferred_element_type=jnp.float32
        ).reshape(kv_dev, own_rows, BLK)
        * score_scale
    )
    live_rows = jnp.repeat(
        jnp.arange(BLK, dtype=jnp.int32)[None, :] < lengths[:, None], group_q, axis=0
    )[None]
    self_scores = (
        jnp.einsum(
            "lhgd,lhd->hlg", own_query, fresh_mine[..., :HD], preferred_element_type=jnp.float32
        ).reshape(kv_dev, own_rows)
        * score_scale
    )
    local_max = jnp.maximum(
        jnp.max(jnp.where(live_rows, tail_scores, neg_big), axis=-1), self_scores
    )
    own_part = lax.dynamic_slice_in_dim(part_max, own_start, own_rows, 1)
    part_max = lax.dynamic_update_slice_in_dim(
        part_max, jnp.maximum(own_part, local_max), own_start, 1
    )
    top_max = lax.pmax(part_max, "node")

    def sum_group(running, group_item):
        run_sum, run_out = running
        group_kv, group_visible = group_item
        scores, keep_mask = masked_scores(group_kv, group_visible)
        weights = jnp.where(keep_mask, jnp.exp(scores - top_max[..., None]), 0.0).astype(
            jnp.bfloat16
        )
        run_sum = run_sum + jnp.sum(weights.astype(jnp.float32), axis=-1)
        run_out = run_out + jnp.einsum(
            "hqk,khd->hqd", weights, group_kv[..., HD:], preferred_element_type=jnp.float32
        )
        return ((run_sum, run_out), None)

    start_state = (
        jnp.zeros((kv_dev, rows_all), jnp.float32),
        jnp.zeros((kv_dev, rows_all, HD), jnp.float32),
    )
    (part_sum, part_out), _ = lax.scan(sum_group, start_state, (cache_groups, visible_groups))
    total_sum, total_out = lax.psum((part_sum, part_out), "node")
    remote_sum = lax.dynamic_slice_in_dim(total_sum, own_start, own_rows, 1)
    remote_out = lax.dynamic_slice_in_dim(total_out, own_start, own_rows, 1)
    full_max = lax.dynamic_slice_in_dim(top_max, own_start, own_rows, 1)
    tail_weights = jnp.where(live_rows, jnp.exp(tail_scores - full_max[..., None]), 0.0).astype(
        jnp.bfloat16
    )
    self_weights = jnp.exp(self_scores - full_max).astype(jnp.bfloat16)
    denominator = (
        remote_sum
        + jnp.sum(tail_weights.astype(jnp.float32), axis=-1)
        + self_weights.astype(jnp.float32)
    )
    tail_part = jnp.einsum(
        "hlgr,lrhd->hlgd",
        tail_weights.reshape(kv_dev, leaf_dev, group_q, BLK),
        tails[..., HD:],
        preferred_element_type=jnp.float32,
    ).reshape(kv_dev, own_rows, HD)
    self_values = (
        jnp.broadcast_to(
            fresh_mine[..., HD:].transpose(1, 0, 2)[:, :, None, :], (kv_dev, leaf_dev, group_q, HD)
        )
        .reshape(kv_dev, own_rows, HD)
        .astype(jnp.float32)
    )
    output = remote_out + tail_part + self_weights.astype(jnp.float32)[..., None] * self_values
    attn_own = (
        (output / denominator[..., None])
        .reshape(kv_dev, leaf_dev, group_q, HD)
        .transpose(1, 0, 2, 3)
    )
    attn_own = attn_own.reshape(leaf_dev, query_cols).astype(jnp.bfloat16)
    attn_all = lax.all_gather(attn_own, "node", axis=0, tiled=True)
    projected_out = lax.psum_scatter(
        jnp.dot(attn_all, w_out, preferred_element_type=jnp.float32),
        "head",
        scatter_dimension=0,
        tiled=True,
    )
    squares = lax.psum(jnp.sum(projected_out * projected_out, axis=1), "node")
    inverse = lax.rsqrt(squares / D + epsilon)
    branch = (projected_out * inverse[:, None] * post_gain[None, :]).astype(jnp.bfloat16)
    row_ids = jnp.arange(BLK, dtype=jnp.int32)[None, :, None, None]
    limit_rows = lengths[:, None, None, None]
    updated = jnp.where(
        row_ids < limit_rows,
        tails,
        jnp.where(row_ids == limit_rows, fresh_mine[:, None], jnp.zeros_like(tails)),
    )
    child_dev = matching.shape[0] // node_count
    my_sources = lax.dynamic_slice_in_dim(matching, node_index * child_dev, child_dev, 0)
    all_tails = lax.all_gather(updated, "node", axis=0, tiled=True)
    children = jnp.take(all_tails, my_sources, axis=0)
    return (branch, children)


def solution(mesh):
    return jax.shard_map(
        shards,
        mesh=mesh,
        in_specs=(
            P(None, "node"),
            P("node", "head"),
            P("node", "head"),
            P("head", "node"),
            P("node"),
            P("node", None, "head", None),
            P("node", None, "head", None),
            P("node"),
            P(),
            P("node"),
            P(),
        ),
        out_specs=(P("head", "node"), P("node", None, "head", None)),
        check_vma=False,
    )
```

profile of v0, /device:TPU:1, one launch (start us, length us, event | category | flops | bytes accessed | tf_op | source)
XLA Modules:
  0.0 846.4 jit_solution(13527808094351792352)
XLA Ops:
  7.3 0.8 copy-done
  8.1 1.1 fusion.21
  9.2 1.1 fusion.22
  10.3 1.0 copy.57
  11.7 219.8 %reduce-scatter.7.cloned.1.call-done = f32[8,512]{1,0:T(8,128)} async-done(((f32[256,512]{1,0:T(8,128)}), f32[8,512]{1,0:T(8,128)}) %reduce-scatter.7.cloned.1.call-update) | async-done | bytes 16400
  231.5 0.9 copy.58
  233.2 28.5 %all_gather.9 = bf16[256,256]{1,0:T(8,128)(2,1)S(1)} all-gather(bf16[8,256]{1,0:T(8,128)(2,1)S(1)} %copy.45), channel_id=1, replica_groups=mesh['node'=32,'head'=16] {'node'}, dimensions={0}, use_global_device_ids=true | all-gather | bytes 135168 | tf_op jit(solution)/shard_map/all_gather | solution.py:52
  261.8 30.3 %while.24 = (s32[]{:T(128)}, f32[1,512]{1,0:T(1,128)S(1)}, pred[6,256,16]{1,2,0:T(8,128)(4,1)S(1)}, bf16[6,1024,1,256]{3,1,2,0:T(8,128)(2,1)}, bf16[1,512,128]{2,1,0:T(8,128)(2,1)S(1)}, /*index=5*/s32[]{:T(128)}, s32[]{:T(128)}) while((s32[]{:T(128)}, f32[1,512]{1,0:T(1,128)S(1)}, pred[6,256,16]{1,2,0:T(8,128)(4,1)S(1)}, ...), condition=%wide.region_3.4_spmd.clone, body=%wide.region_1.3_spmd.clone.sunk | while | flops 135791104 | bytes 5656671 | solution.py:87
  262.4 0.9 broadcast_in_dim.135
  263.3 1.3 reshape.327
  265.3 1.1 dynamic-slice_bitcast_fusion.9
  267.4 0.9 broadcast_in_dim.135
  268.4 1.3 reshape.327
  270.3 1.1 dynamic-slice_bitcast_fusion.9
  272.5 0.9 broadcast_in_dim.135
  273.4 1.3 reshape.327
  275.4 1.1 dynamic-slice_bitcast_fusion.9
  277.5 0.9 broadcast_in_dim.135
  278.5 1.3 reshape.327
  280.4 1.1 dynamic-slice_bitcast_fusion.9
  282.6 0.9 broadcast_in_dim.135
  283.5 1.3 reshape.327
  285.5 1.1 dynamic-slice_bitcast_fusion.9
  287.6 0.9 broadcast_in_dim.135
  288.6 1.3 reshape.327
  290.5 1.1 dynamic-slice_bitcast_fusion.9
  292.3 58.2 %pmax.7 = f32[1,512]{1,0:T(1,128)S(1)} all-reduce(f32[1,512]{1,0:T(1,128)S(1)} %dynamic_update_slice.3), channel_id=1, replica_groups=mesh['node'=32,'head'=16] {'node'}, use_global_device_ids=true, to_apply=%region_5.6 | all-reduce | flops 512 | bytes 4096 | tf_op jit(solution)/shard_map/pmax | solution.py:117
  350.9 34.9 %while.25 = (s32[]{:T(128)}, f32[1,512]{1,0:T(1,128)S(1)}, f32[1,512,128]{2,1,0:T(8,128)S(1)}, pred[6,256,16]{1,2,0:T(8,128)(4,1)S(1)}, bf16[6,1024,1,256]{3,1,2...) while((s32[]{:T(128)}, f32[1,512]{1,0:T(1,128)S(1)}, ...), condition=%wide.region_8.9_spmd.clone, body=%wide.region_6.8_spmd.clone.sunk | while | flops 271712768 | bytes 8542320 | solution.py:136
  350.9 1.1 dynamic-slice_bitcast_fusion.11
  352.6 0.9 broadcast_in_dim.137
  353.5 1.3 reshape.328
  356.8 1.1 dynamic-slice_bitcast_fusion.11
  358.4 0.9 broadcast_in_dim.137
  359.3 1.3 reshape.328
  362.6 1.1 dynamic-slice_bitcast_fusion.11
  364.2 0.9 broadcast_in_dim.137
  365.2 1.3 reshape.328
  367.1 0.8 convert_reduce_fusion.3
  368.4 1.1 dynamic-slice_bitcast_fusion.11
  370.0 0.9 broadcast_in_dim.137
  371.0 1.3 reshape.328
  372.9 0.8 convert_reduce_fusion.3
  374.2 1.1 dynamic-slice_bitcast_fusion.11
  375.8 0.9 broadcast_in_dim.137
  376.8 1.3 reshape.328
  378.8 0.8 convert_reduce_fusion.3
  380.1 1.1 dynamic-slice_bitcast_fusion.11
  381.7 0.9 broadcast_in_dim.137
  382.6 1.3 reshape.328
  384.6 0.8 convert_reduce_fusion.3
  385.9 55.7 %psum.22 = f32[1,512]{1,0:T(1,128)S(1)} all-reduce(f32[1,512]{1,0:T(1,128)S(1)} %get-tuple-element.69), channel_id=1, replica_groups=mesh['node'=32,'head'=16] {'node'}, use_global_device_ids=true, to_apply=%region_10.11 | all-reduce | flops 512 | bytes 4096 | tf_op jit(solution)/shard_map/psum | solution.py:137
  442.0 187.5 %all-reduce.2.cloned.1.call-done = f32[1,512,128]{2,1,0:T(8,128)} async-done(((f32[1,512,128]{2,1,0:T(8,128)}), f32[1,512,128]{2,1,0:T(8,128)}) %all-reduce.2.cloned.1.call-update) | async-done | bytes 262160 | tf_op jit(solution)/shard_map/psum | solution.py:137
  629.6 0.8 fusion.14
  630.3 28.4 %all_gather.10 = bf16[256,256]{1,0:T(8,128)(2,1)S(1)} all-gather(bf16[8,256]{1,0:T(8,128)(2,1)S(1)} %convert_element_type.75), channel_id=1, replica_groups=mesh['node'=32,'head'=16] {'node'}, dimensions={0}, use_global_device_ids=true | all-gather | bytes 135168 | tf_op jit(solution)/shard_map/all_gather | solution.py:170
  658.7 0.9 fusion.24
  659.8 0.9 select_select_fusion
  660.8 0.8 compare_and_fusion
  661.5 66.3 %reduce-scatter.5.cloned.1.call-done = f32[16,168]{1,0:T(8,128)} async-done(((f32[256,168]{1,0:T(8,128)}), f32[16,168]{1,0:T(8,128)}) %reduce-scatter.5.cloned.1.call-update) | async-done | bytes 10768 | tf_op jit(solution)/shard_map/reduce_scatter | solution.py:171
  727.8 0.8 multiply_reduce_fusion
  728.7 60.5 %psum.23 = f32[16]{0:T(128)S(1)} all-reduce(f32[16]{0:T(128)S(1)} %multiply_reduce_fusion), channel_id=1, replica_groups=mesh['node'=32,'head'=16] {'node'}, use_global_device_ids=true, to_apply=%region_14.15 | all-reduce | flops 16 | bytes 128 | tf_op jit(solution)/shard_map/psum | solution.py:177
  789.2 1.4 multiply_convert_fusion
  790.6 44.1 %all-gather.2.cloned.1.call-done = bf16[256,64,1,256]{3,1,2,0:T(8,128)(2,1)} async-done(((bf16[8,64,1,256]{3,1,2,0:T(8,128)(2,1)}), bf16[256,64,1,256]{3,1,2,0:T(8,128)(2,1)}) %all-gather.2.cloned.1.call-update) | async-done | bytes 8388624 | tf_op jit(solution)/shard_map/all_gather | solution.py:189
  834.7 4.0 gather_fusion
  838.7 1.1 fusion.7
  (128 shorter events, 23.6 us)
Async XLA Ops:
  7.2 0.9 copy-start
  7.2 4.3 copy-start.5
  7.2 4.3 copy-start.6
  7.2 4.3 copy-start.7
  7.2 225.4 %copy-start.2 = (bf16[8,64,1,256]{3,1,2,0:T(8,128)(2,1)S(1)}, bf16[8,64,1,256]{3,1,2,0:T(8,128)(2,1)}, u32[]{:S(2)}) copy-start(bf16[8,64,1,256]{3,1,2,0:T(8,128)(2,1)} %param.21) | copy-start | bytes 786436
  7.2 224.3 %reduce-scatter.7.cloned.1.call-start = ((), (), s32[]{:S(2)}) async-start(), calls=%async_computation.5 | async-start | bytes 540672
  11.4 618.2 %all-reduce.2.cloned.1.call-start = ((), (), s32[]{:S(2)}) async-start(), calls=%async_computation.2 | async-start | bytes 524288 | tf_op jit(solution)/shard_map/psum | solution.py:137
  350.9 307.8 %copy-start.3 = (bf16[256,168]{0,1:T(8,128)(2,1)S(1)}, bf16[256,168]{0,1:T(8,128)(2,1)}, u32[]{:S(2)}) copy-start(bf16[256,168]{0,1:T(8,128)(2,1)} %param.18) | copy-start | bytes 258052
  385.9 55.7 %copy-start.1 = (f32[1,512,128]{2,1,0:T(8,128)}, f32[1,512,128]{2,1,0:T(8,128)S(1)}, u32[]{:S(2)}) copy-start(f32[1,512,128]{2,1,0:T(8,128)S(1)} %get-tuple-element.68) | copy-start | bytes 786436
  385.9 403.3 %copy-start.4 = (f32[168]{0:T(256)S(1)}, f32[168]{0:T(256)}, u32[]{:S(2)}) copy-start(f32[168]{0:T(256)} %param.19) | copy-start | bytes 2020
  441.6 286.2 %reduce-scatter.5.cloned.1.call-start = ((), (), s32[]{:S(2)}) async-start(), calls=%async_computation.3 | async-start | bytes 278528 | tf_op jit(solution)/shard_map/reduce_scatter | solution.py:171
  659.7 175.0 %all-gather.2.cloned.1.call-start = ((), (), s32[]{:S(2)}) async-start(), calls=%async_computation.4 | async-start | bytes 8650752 | tf_op jit(solution)/shard_map/all_gather | solution.py:189
Sparse Core Ops, SparseCore 0:
  13.0 218.4 reduce-scatter.6
  441.8 187.7 all-reduce.1
  659.8 67.9 reduce-scatter.4
  730.9 103.7 all-gather.1
where the time goes:
time: 847 us; the launch traced here: 846 us
  waiting for transfers between devices  518 us (61%)
  blocking collectives  231 us (27%)
  local copies, waits for them, and re-layouts  61.2 us (7%)
  matrix products  14.5 us (2%)
  between operations  14 us (2%)
    unnamed x5, waiting for transfers between devices  220 us
    psum x1, waiting for transfers between devices, shards(): total_sum, total_out = lax.psum((part_sum, part_out), 'node')  188 us
    reduce_scatter x1, waiting for transfers between devices, shards(): lax.psum_scatter(jnp.dot(attn_all, w_out, preferred_element_type=jnp.floa...  66.3 us
    psum x1, blocking collectives, shards(): squares = lax.psum(jnp.sum(projected_out * projected_out, axis=1), 'node')  60.5 us
    pmax x1, blocking collectives, shards(): top_max = lax.pmax(part_max, 'node')  58.2 us
    psum x1, blocking collectives, shards(): total_sum, total_out = lax.psum((part_sum, part_out), 'node')  55.7 us
    all_gather x1, waiting for transfers between devices, shards(): all_tails = lax.all_gather(updated, 'node', axis=0, tiled=True)  44.1 us
    all_gather x1, blocking collectives, shards(): queries = lax.all_gather(query_mine, 'node', axis=0, tiled=True)  28.5 us
  transfers between devices with their start and end apart: 4, of which 4 were waited for; matrix products, arithmetic and copies ran while one was open for 1% of the time, Pallas kernels for 0%

commit v1 on v0

v1 whole, which is shorter than its diff:
```python
import functools
import math

import jax
import jax.numpy as jnp
from jax import lax
from jax.experimental import pallas as pl
from jax.experimental.pallas import tpu as pltpu
from jax.sharding import PartitionSpec as P

D = 5376
HEADS = 32
KVH = 16
HD = 128
BLK = 64
GROUP = HEADS // KVH

score_scale = 168.0 ** (-0.5)
log2_scale = score_scale * math.log2(math.e)
neg_big = -1e30
epsilon = 1e-06
f32 = jnp.float32
bf16 = jnp.bfloat16
CHUNK = 1024
VROWS = HD + 16

VMEM = pl.BlockSpec(memory_space=pltpu.VMEM)
SMEM = pl.BlockSpec(memory_space=pltpu.SMEM)
HBM = pl.BlockSpec(memory_space=pltpu.HBM)


def call(kernel, out_shape, in_specs, out_specs, scratch=(), vmem=8, cost=(0, 0, 0)):
    return pl.pallas_call(
        kernel,
        out_shape=out_shape,
        in_specs=in_specs,
        out_specs=out_specs,
        scratch_shapes=list(scratch),
        compiler_params=pltpu.CompilerParams(vmem_limit_bytes=vmem * 1024 * 1024),
        cost_estimate=pl.CostEstimate(flops=cost[0], bytes_accessed=cost[1], transcendentals=cost[2]),
    )


def matmul_nt(a, b):
    return lax.dot_general(a, b, (((1,), (1,)), ((), ())), preferred_element_type=f32)


def identity(size):
    rows = lax.broadcasted_iota(jnp.int32, (size, size), 0)
    cols = lax.broadcasted_iota(jnp.int32, (size, size), 1)
    return (rows == cols).astype(f32).astype(bf16)


def project_kernel(states_hbm, query_hbm, key_value_hbm, out, states_t, w_query, w_key_value, sems):
    pairs = ((states_hbm, states_t), (query_hbm, w_query), (key_value_hbm, w_key_value))
    copies = [pltpu.make_async_copy(pair[0], pair[1], sems.at[i]) for i, pair in enumerate(pairs)]
    for copy in copies:
        copy.start()
    dims = (((0,), (0,)), ((), ()))
    cols = w_query.shape[1]
    copies[0].wait()
    copies[1].wait()
    out[:, :cols] = lax.dot_general(states_t[...], w_query[...], dims, preferred_element_type=f32)
    copies[2].wait()
    out[:, cols:] = lax.dot_general(states_t[...], w_key_value[...], dims, preferred_element_type=f32)


def home_kernel(parts, rows_rep, fresh):
    total = jnp.sum(parts[...], axis=0)
    pair = jnp.concatenate([total, total], axis=0).astype(bf16)
    for index in range(rows_rep.shape[0] // 16):
        rows_rep[pl.ds(index * 16, 16), :] = pair
    fresh[...] = total[:, total.shape[1] // 2 :]


def attend_kernel(
    rows_hbm,
    cache_hbm,
    tails_hbm,
    fresh_hbm,
    ancestry_hbm,
    block_node_hbm,
    lengths_hbm,
    out,
    scores,
    values_t,
    updated,
    bias,
    cache,
    queries,
    tails,
    fresh,
    ancestry,
    block_node,
    lengths,
    sems,
):
    node = lax.axis_index("node")
    leaves = queries.shape[0]
    cached = cache.shape[0]
    steps = range(0, cached, CHUNK)
    pairs = [
        (ancestry_hbm, ancestry),
        (block_node_hbm, block_node),
        (lengths_hbm, lengths),
        (tails_hbm, tails),
        (fresh_hbm, fresh),
        (rows_hbm.at[:, pl.ds(0, queries.shape[1])], queries),
    ]
    pairs += [(cache_hbm.at[pl.ds(start, CHUNK), :], cache.at[pl.ds(start, CHUNK), :]) for start in steps]
    copies = [pltpu.make_async_copy(pair[0], pair[1], sems.at[i]) for i, pair in enumerate(pairs)]
    for copy in copies:
        copy.start()
    for copy in copies[:2]:
        copy.wait()
    nodes_all = ancestry.shape[1]
    tree = lax.broadcasted_iota(jnp.int32, (nodes_all, block_node.shape[1]), 0)
    one_hot = (tree == block_node[...]).astype(f32).astype(bf16)
    seen = lax.dot_general(
        one_hot,
        ancestry[...].astype(f32).astype(bf16),
        (((0,), (1,)), ((), ())),
        preferred_element_type=f32,
    )
    shut = jnp.where(seen > 0.5, 0.0, neg_big)
    for g in range(GROUP):
        bias[:, g * leaves : (g + 1) * leaves] = shut
    eye = identity(HD)
    values_t[HD:, :] = jnp.ones((VROWS - HD, values_t.shape[1]), bf16)
    for copy in copies[2:5]:
        copy.wait()
    leaf_dev = fresh.shape[0]
    lanes = lax.broadcasted_iota(jnp.int32, lengths.shape, 1)
    length = [
        jnp.sum(jnp.where(lanes == leaf, lengths[...], 0).astype(f32), axis=1, keepdims=True)
        for leaf in range(leaf_dev)
    ]
    rows = lax.broadcasted_iota(jnp.int32, (BLK, 2 * HD), 0).astype(f32)
    for leaf in range(leaf_dev):
        span = pl.ds(leaf * BLK, BLK)
        block = jnp.where(rows < length[leaf], tails[span, :].astype(f32), 0.0)
        block = jnp.where(rows == length[leaf], fresh[leaf : leaf + 1, :], block)
        updated[span, :] = block.astype(bf16)
    values_t[:HD, cached:] = matmul_nt(eye, updated[:, HD:]).astype(bf16)
    rows_all = leaves * GROUP
    copies[5].wait()
    query = jnp.concatenate([queries[:, HD * g : HD * (g + 1)] for g in range(GROUP)], axis=0)
    own = updated.shape[0]
    top = jnp.full((8, rows_all), neg_big, f32)
    lanes = lax.broadcasted_iota(jnp.int32, (BLK, rows_all), 1) % leaves
    rows = lax.broadcasted_iota(jnp.int32, (BLK, rows_all), 0).astype(f32)
    raw = matmul_nt(updated[:, :HD], query)
    for leaf in range(leaf_dev):
        keep = (lanes == node * leaf_dev + leaf) & (rows <= length[leaf])
        part = jnp.where(keep, raw[leaf * BLK : (leaf + 1) * BLK] * log2_scale, neg_big)
        scores[pl.ds(cached + leaf * BLK, BLK), :] = part
        top = jnp.maximum(top, jnp.max(part.reshape(BLK // 8, 8, rows_all), axis=0))
    for step, start in enumerate(steps):
        copies[6 + step].wait()
        values_t[:HD, start : start + CHUNK] = matmul_nt(eye, cache[start : start + CHUNK, HD:]).astype(bf16)
        raw = matmul_nt(cache[start : start + CHUNK, :HD], query)
        for block in range(CHUNK // BLK):
            at = start // BLK + block
            part = raw[block * BLK : (block + 1) * BLK] * log2_scale + bias[at : at + 1, :]
            scores[pl.ds(start + block * BLK, BLK), :] = part
            top = jnp.maximum(top, jnp.max(part.reshape(BLK // 8, 8, rows_all), axis=0))
    row_max = jnp.max(top, axis=0, keepdims=True)
    total = jnp.zeros((VROWS, rows_all), f32)
    for start in range(0, cached + own, CHUNK):
        stop = min(start + CHUNK, cached + own)
        weights = jnp.exp2(scores[start:stop, :] - row_max).astype(bf16)
        total = total + jnp.dot(values_t[:, start:stop], weights, preferred_element_type=f32)
    weight_sum = total[HD : HD + 1]
    mean_t = (total[:HD] / weight_sum).astype(bf16)
    level = row_max + jnp.log2(weight_sum)
    high = level.astype(bf16).astype(f32)
    middle = (level - high).astype(bf16).astype(f32)
    low = level - high - middle
    index = lax.broadcasted_iota(jnp.int32, (HD, rows_all), 0)
    level_t = jnp.where(index == 0, high, jnp.where(index == 1, middle, jnp.where(index == 2, low, 0.0)))
    for leaf in range(leaf_dev):
        level_t = jnp.where(index == 3 + leaf, length[leaf], level_t)
    level_t = level_t.astype(bf16)
    eye = identity(leaves)
    nodes = out.shape[0]
    for part, array in enumerate((mean_t, level_t)):
        turned = [
            matmul_nt(eye, array[:, g * leaves : (g + 1) * leaves]).reshape(nodes, leaf_dev, HD)
            for g in range(GROUP)
        ]
        span = GROUP * leaf_dev
        out[:, part * span : (part + 1) * span, :] = jnp.concatenate(turned, axis=1).astype(bf16)


def combine_kernel(parts, out):
    span = parts.shape[1] // 2
    mean = parts[:, :span, :].astype(f32)
    level = parts[:, span:, :].astype(f32)
    lanes = lax.broadcasted_iota(jnp.int32, level.shape, 2)
    level = jnp.sum(jnp.where(lanes < 3, level, 0.0), axis=2, keepdims=True)
    top = jnp.max(level, axis=0, keepdims=True)
    weight = jnp.broadcast_to(jnp.exp2(level - top), mean.shape)
    result = jnp.sum(weight * mean, axis=0) / jnp.sum(weight, axis=0)
    leaf_dev = span // GROUP
    mine = jnp.concatenate([result[g * leaf_dev : (g + 1) * leaf_dev] for g in range(GROUP)], axis=1)
    pair = jnp.concatenate([mine, mine], axis=0).astype(bf16)
    for index in range(out.shape[0] // 16):
        out[pl.ds(index * 16, 16), :] = pair


def output_kernel(attention, w_out_t, partial):
    partial[...] = matmul_nt(attention[...], w_out_t[...]).astype(bf16)


def square_kernel(partial, projected, squares):
    total = jnp.sum(partial[...].astype(f32), axis=0)
    projected[...] = total
    sums = jnp.sum(total * total, axis=1, keepdims=True)
    leaves = total.shape[0]
    rows = lax.broadcasted_iota(jnp.int32, (leaves, HD), 0)
    cols = lax.broadcasted_iota(jnp.int32, (leaves, HD), 1)
    line = jnp.sum(jnp.where(rows == cols, sums, 0.0), axis=0, keepdims=True)
    squares[...] = jnp.broadcast_to(line, squares.shape)


def scale_kernel(squares, projected, gain, branch):
    leaves = projected.shape[0]
    line = jnp.sum(squares[...], axis=0, keepdims=True)
    rows = lax.broadcasted_iota(jnp.int32, (leaves, HD), 0)
    cols = lax.broadcasted_iota(jnp.int32, (leaves, HD), 1)
    sums = jnp.sum(jnp.where(rows == cols, line, 0.0), axis=1, keepdims=True)
    inverse = lax.rsqrt(sums / D + epsilon)
    branch[...] = (projected[...] * inverse * gain[...]).astype(bf16)


def children_kernel(leaf_dev, sources, tails, rows_all, levels, out, blocks, fresh, lens, sems):
    count = out.shape[0]
    copies = []
    for index in range(count):
        copy = pltpu.make_async_copy(tails.at[sources[index]], blocks.at[index], sems.at[index])
        copy.start()
        copies.append(copy)
    span = levels.shape[1] // 2
    fresh[...] = rows_all[:, rows_all.shape[1] // 2 :].astype(f32)
    lens[...] = jnp.max(levels[:, span:, :].astype(f32), axis=1)
    rows = lax.broadcasted_iota(jnp.int32, (BLK, 2 * HD), 0).astype(f32)
    lanes = lax.broadcasted_iota(jnp.int32, (1, HD), 1)
    for index in range(count):
        leaf = sources[index]
        line = lens[pl.ds(leaf // leaf_dev, 1), :]
        length = jnp.sum(jnp.where(lanes == 3 + leaf % leaf_dev, line, 0.0), axis=1, keepdims=True)
        copies[index].wait()
        block = jnp.where(rows < length, blocks[index].astype(f32), 0.0)
        block = jnp.where(rows == length, fresh[pl.ds(leaf, 1), :], block)
        out[index] = block.astype(bf16)


def shards(
    states,
    w_query,
    w_key_value,
    w_out,
    post_gain,
    cache,
    tails,
    lengths,
    ancestry,
    block_node,
    matching,
):
    nodes = lax.axis_size("node")
    heads = lax.axis_size("head")
    node = lax.axis_index("node")
    leaves = states.shape[0]
    leaf_dev = leaves // nodes
    query_cols = w_query.shape[1]
    all_cols = query_cols + w_key_value.shape[1]
    columns = w_out.shape[1]
    rows_all = leaves * GROUP
    child_dev = matching.shape[0] // nodes
    shape = jax.ShapeDtypeStruct

    cache_rows = cache.reshape(-1, 2 * HD)
    tail_rows = tails.reshape(-1, 2 * HD)
    key_count = cache_rows.shape[0]
    extended = key_count + leaf_dev * BLK
    all_tails = lax.all_gather(tail_rows, "node", axis=0, tiled=True)

    partial = call(
        project_kernel,
        shape((leaves, all_cols), f32),
        [HBM] * 3,
        VMEM,
        [
            pltpu.VMEM((states.shape[1], leaves), bf16),
            pltpu.VMEM(w_query.shape, bf16),
            pltpu.VMEM(w_key_value.shape, bf16),
            pltpu.SemaphoreType.DMA((3,)),
        ],
        vmem=60,
        cost=(2 * leaves * all_cols * states.shape[1], 1000000, 0),
    )(states.T, w_query, w_key_value)
    parts = lax.all_to_all(partial.reshape(nodes, leaf_dev, all_cols), "node", 0, 0, tiled=True)

    rows_rep, fresh = call(
        home_kernel,
        (shape((leaves, all_cols), bf16), shape((leaf_dev, 2 * HD), f32)),
        [VMEM],
        (VMEM, VMEM),
        cost=(leaves * all_cols, 4 * leaves * all_cols, 0),
    )(parts)
    rows = lax.all_to_all(rows_rep.reshape(nodes, leaf_dev, all_cols), "node", 0, 0, tiled=True)
    rows = rows.reshape(leaves, all_cols)
    span = 2 * GROUP * leaf_dev
    sent = call(
        attend_kernel,
        shape((nodes, span, HD), bf16),
        [HBM] * 7,
        VMEM,
        [
            pltpu.VMEM((extended, rows_all), f32),
            pltpu.VMEM((VROWS, extended), bf16),
            pltpu.VMEM((leaf_dev * BLK, 2 * HD), bf16),
            pltpu.VMEM((block_node.shape[0], rows_all), f32),
            pltpu.VMEM(cache_rows.shape, bf16),
            pltpu.VMEM((leaves, query_cols), bf16),
            pltpu.VMEM(tail_rows.shape, bf16),
            pltpu.VMEM(fresh.shape, f32),
            pltpu.VMEM(ancestry.shape, jnp.int32),
            pltpu.VMEM((1, block_node.shape[0]), jnp.int32),
            pltpu.VMEM((1, leaf_dev), jnp.int32),
            pltpu.SemaphoreType.DMA((6 + key_count // CHUNK,)),
        ],
        vmem=60,
        cost=(4 * rows_all * extended * HD, 8 * HD * key_count, rows_all * extended),
    )(
        rows,
        cache_rows,
        tail_rows,
        fresh,
        ancestry,
        block_node.reshape(1, -1),
        lengths.reshape(1, -1),
    )
    landed = lax.all_to_all(sent, "node", 0, 0, tiled=True)
    mine = call(
        combine_kernel,
        shape((leaves, query_cols), bf16),
        [VMEM],
        VMEM,
        cost=(10 * rows_all * HD, 4 * rows_all * HD, rows_all * HD),
    )(landed)
    attention = lax.all_to_all(mine.reshape(nodes, leaf_dev, query_cols), "node", 0, 0, tiled=True)
    leaf_out = leaves // heads
    partial_out = call(
        output_kernel,
        shape((leaves, columns), bf16),
        [VMEM, VMEM],
        VMEM,
        cost=(2 * leaves * columns * query_cols, 6 * columns * query_cols, 0),
    )(attention.reshape(leaves, query_cols), w_out.T)
    partial_out = lax.all_to_all(
        partial_out.reshape(heads, leaf_out, columns), "head", 0, 0, tiled=True
    )
    projected, squares = call(
        square_kernel,
        (shape((leaf_out, columns), f32), shape((nodes, HD), f32)),
        [VMEM],
        (VMEM, VMEM),
        cost=(leaves * columns, 4 * leaves * columns, 0),
    )(partial_out)
    squares = lax.all_to_all(squares.reshape(nodes, 1, HD), "node", 0, 0, tiled=True)
    sources = lax.dynamic_slice_in_dim(matching, node * child_dev, child_dev, 0)
    children = call(
        functools.partial(children_kernel, leaf_dev),
        shape((child_dev, BLK, 2 * HD), bf16),
        [SMEM, HBM, VMEM, VMEM],
        VMEM,
        [
            pltpu.VMEM((child_dev, BLK, 2 * HD), bf16),
            pltpu.VMEM((leaves, 2 * HD), f32),
            pltpu.VMEM((nodes, HD), f32),
            pltpu.SemaphoreType.DMA((child_dev,)),
        ],
        vmem=60,
        cost=(1000000, 4 * child_dev * BLK * 2 * HD, 0),
    )(sources, all_tails.reshape(leaves, BLK, 2 * HD), rows, landed)
    squares, children = lax.optimization_barrier((squares, children))
    branch = call(
        scale_kernel,
        shape((leaf_out, columns), bf16),
        [VMEM] * 3,
        VMEM,
    )(squares.reshape(nodes, HD), projected, post_gain.reshape(1, columns))
    return (branch, children.reshape(child_dev, BLK, 1, 2 * HD))


def solution(mesh):
    return jax.shard_map(
        shards,
        mesh=mesh,
        in_specs=(
            P(None, "node"),
            P("node", "head"),
            P("node", "head"),
            P("head", "node"),
            P("node"),
            P("node", None, "head", None),
            P("node", None, "head", None),
            P("node"),
            P(),
            P("node"),
            P(),
        ),
        out_specs=(P("head", "node"), P("node", None, "head", None)),
        check_vma=False,
    )
```

time: 847 us -> 145 us (0.17)
  waiting for transfers between devices: 518 us -> 2.21 us
  blocking collectives: 231 us -> 104 us
  local copies, waits for them, and re-layouts: 61.2 us -> 1.29 us
  Pallas kernels: 0 us -> 18.4 us
  matrix products: 14.5 us -> 0 us
    unnamed x5 -> x1, waiting for transfers between devices: 220 us -> 0.68 us
    psum x1 -> x0, waiting for transfers between devices: 188 us -> none  [shards(): total_sum, total_out = lax.psum((part_sum, part_out), 'node')]
    psum x2 -> x0, blocking collectives: 116 us -> none  [the longest x1 60.5 us: shards(): squares = lax.psum(jnp.sum(projected_out * projected_out, axis=1), 'node')]
    all_to_all x0 -> x5, blocking collectives: none -> 104 us  [the longest x1 29.1 us: shards(): lax.all_to_all(partial_out.reshape(heads, leaf_out, columns), 'head', 0,...]
    reduce_scatter x1 -> x0, waiting for transfers between devices: 66.3 us -> none  [shards(): lax.psum_scatter(jnp.dot(attn_all, w_out, preferred_element_type=jnp.floa...]
    pmax x1 -> x0, blocking collectives: 58.2 us -> none  [shards(): top_max = lax.pmax(part_max, 'node')]
    all_gather x2 -> x0, blocking collectives: 56.9 us -> none  [the longest x1 28.5 us: shards(): queries = lax.all_gather(query_mine, 'node', axis=0, tiled=True)]
    all_gather x1, waiting for transfers between devices: 44.1 us -> 0.01 us  [shards(): all_tails = lax.all_gather(tail_rows, 'node', axis=0, tiled=True)]
  transfers between devices with their start and end apart: 4 -> 2, of which waited for: 4 -> 1; matrix products, arithmetic and copies ran while one was open for 1% -> 1% of each run, Pallas kernels for 0% -> 12%
where the time goes in v1:
time: 145 us; the launch traced here: 144 us
  blocking collectives  104 us (72%)
  Pallas kernels  18.4 us (13%)
  between operations  14.1 us (10%)
  starting transfers between devices  4.09 us (3%)
  waiting for transfers between devices  2.21 us (2%)
    all_to_all x1, blocking collectives, shards(): lax.all_to_all(partial_out.reshape(heads, leaf_out, columns), 'head', 0,...  29.1 us
    all_to_all x1, blocking collectives, shards(): lax.all_to_all(partial.reshape(nodes, leaf_dev, all_cols), 'node', 0, 0,...  24.8 us
    all_to_all x1, blocking collectives, shards(): landed = lax.all_to_all(sent, 'node', 0, 0, tiled=True)  18.1 us
    all_to_all x1, blocking collectives, shards(): lax.all_to_all(rows_rep.reshape(nodes, leaf_dev, all_cols), 'node', 0, 0,...  17.8 us
    all_to_all x1, blocking collectives, shards(): lax.all_to_all(mine.reshape(nodes, leaf_dev, query_cols), 'node', 0, 0, t...  14.4 us
    pallas_call x1, Pallas kernels, shards(): call(attend_kernel, shape((nodes, span, HD), bf16), [HBM] * 7, VMEM, [plt...  8.44 us
    pallas_call x1, Pallas kernels, shards(): call(functools.partial(children_kernel, leaf_dev), shape((child_dev, BLK,...  5.81 us
    all_to_all x1, starting transfers between devices, shards(): lax.all_to_all(squares.reshape(nodes, 1, HD), 'node', 0, 0, tiled=True)  4.06 us
  transfers between devices with their start and end apart: 2, of which 1 were waited for; matrix products, arithmetic and copies ran while one was open for 1% of the time, Pallas kernels for 12%

profile of v1, /device:TPU:1, one launch (start us, length us, event | category | flops | bytes accessed | tf_op | source)
XLA Modules:
  0.0 144.3 jit_solution(10056844636910194552)
XLA Ops:
  7.2 0.0 copy-start.1
  7.2 0.0 all-gather.2.cloned.1.call-start
  7.2 0.7 all-gather.2.cloned.1.call-update
  7.9 2.2 %shard_map.122 = f32[256,512]{1,0:T(8,128)} custom-call(bf16[168,256]{1,0:T(8,128)(2,1)} %bitcast.35, bf16[168,256]{1,0:T(8,128)(2,1)} %query_hbm.1, bf16[168,256]{1,0:T(8,128)(2,1)} %key_value_hbm.1), custom_call_target="tpu_custom_call" | custom-call | flops 44040192 | bytes 1000000 | tf_op jit(solution)/shard_map/pallas_call | solution.py:289
  10.1 24.8 %all_to_all.30.parts = f32[32,8,512]{2,1,0:T(8,128)S(1)} all-to-all(f32[32,8,512]{2,1,0:T(8,128)} %bitcast.29), channel_id=1, replica_groups=mesh['node'=32,'head'=16] {'node'}, dimensions={0} | all-to-all | bytes 1048576 | tf_op jit(solution)/shard_map/all_to_all | solution.py:303
  35.0 0.1 shard_map.123
  35.0 0.0 copy-start.3
  35.0 17.8 %all_to_all.31 = bf16[32,8,512]{2,1,0:T(8,128)(2,1)} all-to-all(bf16[32,8,512]{2,1,0:T(8,128)(2,1)S(1)} %bitcast.24), channel_id=1, replica_groups=mesh['node'=32,'head'=16] {'node'}, dimensions={0} | all-to-all | bytes 524288 | tf_op jit(solution)/shard_map/all_to_all | solution.py:312
  52.8 0.0 copy-done.3
  52.8 0.0 copy-start.2
  52.8 8.4 %shard_map.124 = bf16[32,32,128]{2,1,0:T(8,128)(2,1)} custom-call(bf16[256,512]{1,0:T(8,128)(2,1)} %bitcast.31, bf16[6144,256]{1,0:T(8,128)(2,1)} %bitcast.36, bf16[512,256]{1,0:T(8,128)(2,1)} %bitcast.34, f32[8,256]{1,0:T(8,128)} %copy-done.3, s32[256,128]{1,0:T(8,128)} %ancestry_hbm.1, s32[1,96]{1,0:T(1,128)} %bitcast.37, s32[1,8]{1,0:T(1,128)} %bitcast.38), custom_call_target="tpu_custom_call" | custom-call | flops 1744830464 | bytes 6291456 | tf_op jit(solution)/shard_map/pallas_call | solution.py:315
  61.3 18.1 %all_to_all.32.parts.levels = bf16[32,32,128]{2,1,0:T(8,128)(2,1)S(1)} all-to-all(bf16[32,32,128]{2,1,0:T(8,128)(2,1)} %shard_map.124), channel_id=1, replica_groups=mesh['node'=32,'head'=16] {'node'}, dimensions={0} | all-to-all | bytes 524288 | tf_op jit(solution)/shard_map/all_to_all | solution.py:345
  79.3 0.0 copy-start
  79.3 0.2 shard_map.125
  79.6 14.4 %all_to_all.33 = bf16[32,8,256]{2,1,0:T(8,128)(2,1)S(1)} all-to-all(bf16[32,8,256]{2,1,0:T(8,128)(2,1)S(1)} %bitcast.21), channel_id=1, replica_groups=mesh['node'=32,'head'=16] {'node'}, dimensions={0} | all-to-all | bytes 262144 | tf_op jit(solution)/shard_map/all_to_all | solution.py:353
  94.0 0.0 copy-done.1
  94.0 0.2 shard_map.126
  94.2 29.1 %all_to_all.34.partial = bf16[16,16,168]{2,1,0:T(8,128)(2,1)S(1)} all-to-all(bf16[16,16,168]{2,1,0:T(8,128)(2,1)S(1)} %bitcast.23), channel_id=1, replica_groups=mesh['node'=32,'head'=16] {'head'}, dimensions={0} | all-to-all | bytes 172032 | tf_op jit(solution)/shard_map/all_to_all | solution.py:362
  123.3 0.7 shard_map.127
  124.0 4.1 %all-to-all-start.5 = ((f32[32,1,128]{2,1,0:T(1,128)}), f32[32,1,128]{2,1,0:T(1,128)S(1)}, u32[]{:S(2)}, u32[]{:S(2)}) async-start(f32[32,1,128]{2,1,0:T(1,128)} %bitcast.13), calls=%async_computation.5 | async-start | bytes 32768 | tf_op jit(solution)/shard_map/all_to_all | solution.py:372
  128.1 1.3 dynamic_slice.3.sources
  129.4 0.0 all-gather.2.cloned.1.call-done
  129.4 0.0 copy-done
  129.4 5.8 %shard_map.128 = bf16[32,64,256]{2,1,0:T(8,128)(2,1)} custom-call(s32[32]{0:T(128)} %dynamic_slice.3.sources, bf16[256,64,256]{2,1,0:T(8,128)(2,1)} %bitcast.28, bf16[256,512]{1,0:T(8,128)(2,1)} %bitcast.32, bf16[32,32,128]{2,1,0:T(8,128)(2,1)} %copy-done), custom_call_target="tpu_custom_call" | custom-call | flops 1000000 | bytes 2097152 | tf_op jit(solution)/shard_map/pallas_call | solution.py:374
  135.2 1.5 %all-to-all-done.5 = f32[32,1,128]{2,1,0:T(1,128)S(1)} async-done(((f32[32,1,128]{2,1,0:T(1,128)}), f32[32,1,128]{2,1,0:T(1,128)S(1)}, u32[]{:S(2)}, u32[]{:S(2)}) %all-to-all-start.5) | async-done | bytes 16416 | tf_op jit(solution)/shard_map/all_to_all | solution.py:372
  136.7 0.0 copy-done.2
  136.7 0.7 shard_map.129
Async XLA Ops:
  7.2 86.8 %copy-start.1 = (bf16[256,168]{0,1:T(8,128)(2,1)S(1)}, bf16[256,168]{0,1:T(8,128)(2,1)}, u32[]{:S(2)}) copy-start(bf16[256,168]{0,1:T(8,128)(2,1)} %param.14) | copy-start | bytes 258052
  7.2 122.2 %all-gather.2.cloned.1.call-start = ((), (), s32[]{:S(2)}) async-start(), calls=%async_computation.6 | async-start | bytes 8650752 | tf_op jit(solution)/shard_map/all_gather | solution.py:287
  35.0 17.8 %copy-start.3 = (f32[8,256]{1,0:T(8,128)}, f32[8,256]{1,0:T(8,128)S(1)}, u32[]{:S(2)}) copy-start(f32[8,256]{1,0:T(8,128)S(1)} %get-tuple-element.9.fresh_hbm) | copy-start | bytes 24580
  52.8 83.9 %copy-start.2 = (f32[168]{0:T(256)S(1)}, f32[168]{0:T(256)}, u32[]{:S(2)}) copy-start(f32[168]{0:T(256)} %param.15) | copy-start | bytes 2020
  79.3 50.0 %copy-start = (bf16[32,32,128]{2,1,0:T(8,128)(2,1)}, bf16[32,32,128]{2,1,0:T(8,128)(2,1)S(1)}, u32[]{:S(2)}) copy-start(bf16[32,32,128]{2,1,0:T(8,128)(2,1)S(1)} %all_to_all.32.parts.levels) | copy-start | bytes 786436
  124.0 12.7 %all-to-all-start.5 = ((f32[32,1,128]{2,1,0:T(1,128)}), f32[32,1,128]{2,1,0:T(1,128)S(1)}, u32[]{:S(2)}, u32[]{:S(2)}) async-start(f32[32,1,128]{2,1,0:T(1,128)} %bitcast.13), calls=%async_computation.5 | async-start | bytes 32768 | tf_op jit(solution)/shard_map/all_to_all | solution.py:372
Sparse Core Ops, SparseCore 0:
  11.2 113.3 all-gather.1

commit v2 on v1

v2 whole, which is shorter than its diff:
```python
import math

import jax
import jax.numpy as jnp
from jax import lax
from jax.experimental import pallas as pl
from jax.experimental.pallas import tpu as pltpu
from jax.sharding import PartitionSpec as P

D = 5376
HEADS = 32
KVH = 16
HD = 128
BLK = 64
GROUP = HEADS // KVH

score_scale = 168.0 ** (-0.5)
log2_scale = score_scale * math.log2(math.e)
neg_big = -1e30
epsilon = 1e-06
f32 = jnp.float32
bf16 = jnp.bfloat16
CHUNK = 3072
VROWS = HD + 16
FIRST = 56
SECOND = 8

VMEM = pl.BlockSpec(memory_space=pltpu.VMEM)
SMEM = pl.BlockSpec(memory_space=pltpu.SMEM)
HBM = pl.BlockSpec(memory_space=pltpu.HBM)


def call(kernel, out_shape, in_specs, out_specs, scratch=(), vmem=8, cost=(0, 0, 0)):
    return pl.pallas_call(
        kernel,
        out_shape=out_shape,
        in_specs=in_specs,
        out_specs=out_specs,
        scratch_shapes=list(scratch),
        compiler_params=pltpu.CompilerParams(vmem_limit_bytes=vmem * 1024 * 1024),
        cost_estimate=pl.CostEstimate(flops=cost[0], bytes_accessed=cost[1], transcendentals=cost[2]),
    )


def matmul_nt(a, b):
    return lax.dot_general(a, b, (((1,), (1,)), ((), ())), preferred_element_type=f32)


def identity(size):
    rows = lax.broadcasted_iota(jnp.int32, (size, size), 0)
    cols = lax.broadcasted_iota(jnp.int32, (size, size), 1)
    return (rows == cols).astype(f32).astype(bf16)


def halves(value):
    high = value.astype(bf16)
    return high, (value - high.astype(f32)).astype(bf16)


def project_kernel(
    states_hbm, query_hbm, key_value_hbm, matching_hbm, out, picks, states_t, w_query, w_key_value, matching, sems
):
    pairs = (
        (states_hbm, states_t),
        (query_hbm, w_query),
        (key_value_hbm, w_key_value),
        (matching_hbm, matching),
    )
    copies = [pltpu.make_async_copy(pair[0], pair[1], sems.at[i]) for i, pair in enumerate(pairs)]
    for copy in copies:
        copy.start()
    dims = (((0,), (0,)), ((), ()))
    cols = w_query.shape[1]
    copies[0].wait()
    copies[1].wait()
    query = lax.dot_general(states_t[...], w_query[...], dims, preferred_element_type=f32)
    out[:, :cols], out[:, cols : 2 * cols] = halves(query)
    copies[2].wait()
    fresh = lax.dot_general(states_t[...], w_key_value[...], dims, preferred_element_type=f32)
    key, rest = halves(fresh[:, :HD])
    out[:, 2 * cols :] = jnp.concatenate([key, rest, fresh[:, HD:].astype(bf16)], axis=1)
    copies[3].wait()
    node = lax.axis_index("node")
    child_dev = matching.shape[0] * HD // lax.axis_size("node")
    leaf_dev = states_t.shape[1] // lax.axis_size("node")
    parent = matching[...]
    first = node * leaf_dev
    own = (parent >= first) & (parent < first + leaf_dev)
    part = jnp.where(own, parent - first, 0).astype(f32).astype(bf16)
    of = lax.broadcasted_iota(jnp.int32, (HD, HD), 0) // child_dev
    to = lax.broadcasted_iota(jnp.int32, (HD, HD), 1) // child_dev
    same = (of == to).astype(f32).astype(bf16)
    picks[...] = jnp.dot(part, same, preferred_element_type=f32).astype(jnp.int32)


def home_kernel(
    parts_hbm,
    tails_hbm,
    lengths_hbm,
    picks_hbm,
    sends,
    updated,
    second,
    parts,
    tails,
    lengths,
    blocks,
    picks,
    sems,
):
    pairs = (
        (parts_hbm, parts),
        (lengths_hbm, lengths),
        (tails_hbm, tails),
        (picks_hbm, picks),
    )
    copies = [pltpu.make_async_copy(pair[0], pair[1], sems.at[i]) for i, pair in enumerate(pairs)]
    for copy in copies:
        copy.start()
    copies[1].wait()
    length = leaf_lengths(lengths)
    copies[0].wait()
    leaf_dev = lengths.shape[1]
    total = jnp.sum(parts[...].astype(f32).reshape(-1, leaf_dev, parts.shape[1]), axis=0)
    cols = GROUP * HD
    query = (total[:, :cols] + total[:, cols : 2 * cols]).astype(bf16).astype(f32)
    total = total[:, 2 * cols :]
    fresh = jnp.concatenate([total[:, :HD] + total[:, HD : 2 * HD], total[:, 2 * HD :]], axis=1)
    rows = lax.broadcasted_iota(jnp.int32, (BLK, 2 * HD), 0).astype(f32)
    copies[2].wait()
    for leaf in range(leaf_dev):
        span = pl.ds(leaf * BLK, BLK)
        block = jnp.where(rows < length[leaf], tails[span, :].astype(f32), 0.0)
        block = jnp.where(rows == length[leaf], fresh[leaf : leaf + 1], block)
        block = block.astype(bf16)
        updated[span, :] = block
        blocks[span, :] = block.astype(f32)
    copies[3].wait()
    for index in range(sends.shape[0]):
        start = pl.multiple_of(pick_of(picks, index, sends.shape[0]) * BLK, BLK)
        block = blocks[pl.ds(start, BLK), :]
        sends[index] = jnp.concatenate([query, block[:FIRST]], axis=0).astype(bf16)
        second[index] = jnp.concatenate([query, block[FIRST:]], axis=0).astype(bf16)


def pick_of(picks, index, count):
    line = HD * picks.shape[0] // count
    return picks[index * line // HD, index * line % HD]


def leaf_lengths(lengths):
    lanes = lax.broadcasted_iota(jnp.int32, lengths.shape, 1)
    return [
        jnp.sum(jnp.where(lanes == leaf, lengths[...], 0).astype(f32), axis=1, keepdims=True)
        for leaf in range(lengths.shape[1])
    ]


def attend_kernel(
    rows_hbm,
    cache_hbm,
    updated_hbm,
    ancestry_hbm,
    block_node_hbm,
    lengths_hbm,
    out,
    scores,
    values_t,
    updated,
    bias,
    cache,
    rows_in,
    ancestry,
    block_node,
    lengths,
    sems,
):
    node = lax.axis_index("node")
    nodes = rows_in.shape[0]
    leaf_dev = lengths.shape[1]
    leaves = nodes * leaf_dev
    cached = cache.shape[0]
    steps = range(0, cached, CHUNK)
    pairs = [
        (ancestry_hbm, ancestry),
        (block_node_hbm, block_node),
        (lengths_hbm, lengths),
        (updated_hbm, updated),
        (rows_hbm.at[:, pl.ds(0, rows_in.shape[1]), :], rows_in),
    ]
    pairs += [(cache_hbm.at[pl.ds(start, CHUNK), :], cache.at[pl.ds(start, CHUNK), :]) for start in steps]
    copies = [pltpu.make_async_copy(pair[0], pair[1], sems.at[i]) for i, pair in enumerate(pairs)]
    for copy in copies:
        copy.start()
    for copy in copies[:2]:
        copy.wait()
    nodes_all = ancestry.shape[1]
    tree = lax.broadcasted_iota(jnp.int32, (nodes_all, block_node.shape[1]), 0)
    one_hot = (tree == block_node[...]).astype(f32).astype(bf16)
    seen = lax.dot_general(
        one_hot,
        ancestry[...].astype(f32).astype(bf16),
        (((0,), (1,)), ((), ())),
        preferred_element_type=f32,
    )
    shut = jnp.where(seen > 0.5, 0.0, neg_big)
    for g in range(GROUP):
        bias[:, g * leaves : (g + 1) * leaves] = shut
    eye = identity(HD)
    values_t[HD:, :] = jnp.ones((VROWS - HD, values_t.shape[1]), bf16)
    for copy in copies[2:4]:
        copy.wait()
    length = leaf_lengths(lengths)
    values_t[:HD, cached:] = matmul_nt(eye, updated[:, HD:]).astype(bf16)
    rows_all = leaves * GROUP
    copies[4].wait()
    queries = rows_in[...].astype(f32)[:, :leaf_dev, :].reshape(leaves, GROUP * HD)
    query = jnp.concatenate([queries[:, HD * g : HD * (g + 1)] for g in range(GROUP)], axis=0)
    query = query.astype(bf16)
    own = updated.shape[0]
    top = jnp.full((8, rows_all), neg_big, f32)
    lanes = lax.broadcasted_iota(jnp.int32, (BLK, rows_all), 1) % leaves
    rows = lax.broadcasted_iota(jnp.int32, (BLK, rows_all), 0).astype(f32)
    raw = matmul_nt(updated[:, :HD], query)
    for leaf in range(leaf_dev):
        keep = (lanes == node * leaf_dev + leaf) & (rows <= length[leaf])
        part = jnp.where(keep, raw[leaf * BLK : (leaf + 1) * BLK] * log2_scale, neg_big)
        scores[pl.ds(cached + leaf * BLK, BLK), :] = part
        top = jnp.maximum(top, jnp.max(part.reshape(BLK // 8, 8, rows_all), axis=0))
    for step, start in enumerate(steps):
        copies[5 + step].wait()
        values_t[:HD, start : start + CHUNK] = matmul_nt(eye, cache[start : start + CHUNK, HD:]).astype(bf16)
        raw = matmul_nt(cache[start : start + CHUNK, :HD], query)
        for block in range(CHUNK // BLK):
            at = start // BLK + block
            part = raw[block * BLK : (block + 1) * BLK] * log2_scale + bias[at : at + 1, :]
            scores[pl.ds(start + block * BLK, BLK), :] = part
            top = jnp.maximum(top, jnp.max(part.reshape(BLK // 8, 8, rows_all), axis=0))
    row_max = jnp.max(top, axis=0, keepdims=True)
    total = jnp.zeros((VROWS, rows_all), f32)
    for start in range(0, cached + own, CHUNK):
        stop = min(start + CHUNK, cached + own)
        weights = jnp.exp2(scores[start:stop, :] - row_max).astype(bf16)
        total = total + jnp.dot(values_t[:, start:stop], weights, preferred_element_type=f32)
    weight_sum = total[HD : HD + 1]
    mean_t = (total[:HD] / weight_sum).astype(bf16)
    level = row_max + jnp.log2(weight_sum)
    high = level.astype(bf16).astype(f32)
    middle = (level - high).astype(bf16).astype(f32)
    low = level - high - middle
    lines = (nodes * 8, rows_all)
    line = lax.broadcasted_iota(jnp.int32, lines, 0)
    row = lax.broadcasted_iota(jnp.int32, lines, 1)
    part = line % 8
    level = jnp.where(part == 0, high, jnp.where(part == 1, middle, jnp.where(part == 2, low, 0.0)))
    level = jnp.where(row % leaves // leaf_dev == line // 8, level, 0.0).astype(bf16)
    row = lax.broadcasted_iota(jnp.int32, (rows_all, HD), 0)
    lane = lax.broadcasted_iota(jnp.int32, (rows_all, HD), 1)
    gather = (row // leaves * leaf_dev + row % leaf_dev == lane).astype(f32).astype(bf16)
    levels = jnp.dot(level, gather, preferred_element_type=f32).reshape(nodes, 8, HD)
    eye = identity(leaves)
    turned = [
        matmul_nt(eye, mean_t[:, g * leaves : (g + 1) * leaves]).reshape(nodes, leaf_dev, HD)
        for g in range(GROUP)
    ]
    out[...] = jnp.concatenate(turned + [levels], axis=1).astype(bf16)


def combine_kernel(parts, second, out):
    leaf_dev = out.shape[1] - SECOND
    span = GROUP * leaf_dev
    nodes = parts.shape[0]
    both = parts[...].astype(f32)
    mean = both[:, :span, :]
    lines = both[:, span:, :].reshape(nodes * 8, HD).astype(bf16)
    row = lax.broadcasted_iota(jnp.int32, (nodes * span, nodes * 8), 0)
    line = lax.broadcasted_iota(jnp.int32, (nodes * span, nodes * 8), 1)
    spread = ((row // span == line // 8) & (line % 8 < 3)).astype(f32).astype(bf16)
    level = jnp.dot(spread, lines, preferred_element_type=f32).reshape(nodes, span, HD)
    own = lax.broadcasted_iota(jnp.int32, level.shape, 2) == lax.broadcasted_iota(jnp.int32, level.shape, 1)
    level = jnp.sum(jnp.where(own, level, 0.0), axis=2, keepdims=True)
    top = jnp.max(level, axis=0, keepdims=True)
    weight = jnp.broadcast_to(jnp.exp2(level - top), mean.shape)
    result = jnp.sum(weight * mean, axis=0) / jnp.sum(weight, axis=0)
    mine = jnp.concatenate([result[g * leaf_dev : (g + 1) * leaf_dev] for g in range(GROUP)], axis=1)
    for index in range(out.shape[0]):
        rest = second[index].astype(f32)
        out[index] = jnp.concatenate([mine, rest[leaf_dev:]], axis=0).astype(bf16)


def output_kernel(attention, w_out_t, partial):
    nodes = attention.shape[0]
    leaf_dev = attention.shape[1] - SECOND
    rows = attention[:, :16, :].astype(f32)[:, :leaf_dev, :].reshape(nodes * leaf_dev, -1).astype(bf16)
    partial[...] = matmul_nt(rows, w_out_t[...]).astype(bf16)


def square_kernel(partial, projected, squares):
    total = jnp.sum(partial[...].astype(f32), axis=0)
    projected[...] = total
    sums = jnp.sum(total * total, axis=1, keepdims=True)
    leaves = total.shape[0]
    rows = lax.broadcasted_iota(jnp.int32, (leaves, HD), 0)
    cols = lax.broadcasted_iota(jnp.int32, (leaves, HD), 1)
    line = jnp.sum(jnp.where(rows == cols, sums, 0.0), axis=0, keepdims=True)
    squares[...] = jnp.broadcast_to(line, squares.shape)


def scale_kernel(squares, projected, gain, branch):
    leaves = projected.shape[0]
    line = jnp.sum(squares[...], axis=0, keepdims=True)
    rows = lax.broadcasted_iota(jnp.int32, (leaves, HD), 0)
    cols = lax.broadcasted_iota(jnp.int32, (leaves, HD), 1)
    sums = jnp.sum(jnp.where(rows == cols, line, 0.0), axis=1, keepdims=True)
    inverse = lax.rsqrt(sums / D + epsilon)
    branch[...] = (projected[...] * inverse * gain[...]).astype(bf16)


def children_kernel(matching, first, second, out):
    node = lax.axis_index("node")
    count = out.shape[0]
    leaf_dev = first.shape[1] - FIRST
    for index in range(count):
        place = node * count + index
        home = matching[place // HD, place % HD] // leaf_dev
        block = [first[home].astype(f32)[leaf_dev:], second[home].astype(f32)[leaf_dev:]]
        out[index] = jnp.concatenate(block, axis=0).astype(bf16)


def shards(
    states,
    w_query,
    w_key_value,
    w_out,
    post_gain,
    cache,
    tails,
    lengths,
    ancestry,
    block_node,
    matching,
):
    nodes = lax.axis_size("node")
    heads = lax.axis_size("head")
    leaves = states.shape[0]
    leaf_dev = leaves // nodes
    query_cols = w_query.shape[1]
    all_cols = 2 * query_cols + 3 * HD
    columns = w_out.shape[1]
    rows_all = leaves * GROUP
    child_dev = matching.shape[0] // nodes
    shape = jax.ShapeDtypeStruct

    cache_rows = cache.reshape(-1, 2 * HD)
    tail_rows = tails.reshape(-1, 2 * HD)
    key_count = cache_rows.shape[0]
    extended = key_count + leaf_dev * BLK
    matching_lines = matching.reshape(-1, HD)
    length_line = lengths.reshape(1, -1)

    partial, picks = call(
        project_kernel,
        (shape((leaves, all_cols), bf16), shape(matching_lines.shape, jnp.int32)),
        [HBM] * 4,
        (VMEM, VMEM),
        [
            pltpu.VMEM((states.shape[1], leaves), bf16),
            pltpu.VMEM(w_query.shape, bf16),
            pltpu.VMEM(w_key_value.shape, bf16),
            pltpu.VMEM(matching_lines.shape, jnp.int32),
            pltpu.SemaphoreType.DMA((4,)),
        ],
        vmem=60,
        cost=(2 * leaves * all_cols * states.shape[1], 1000000, 0),
    )(states.T, w_query, w_key_value, matching_lines)
    parts = lax.all_to_all(partial.reshape(nodes, leaf_dev, all_cols), "node", 0, 0, tiled=True)

    parts = parts.reshape(leaves, all_cols)
    sends, updated, second = call(
        home_kernel,
        (
            shape((nodes, leaf_dev + FIRST, 2 * HD), bf16),
            shape((leaf_dev * BLK, 2 * HD), bf16),
            shape((nodes, leaf_dev + SECOND, 2 * HD), bf16),
        ),
        [HBM] * 4,
        (VMEM, VMEM, VMEM),
        [
            pltpu.VMEM(parts.shape, bf16),
            pltpu.VMEM(tail_rows.shape, bf16),
            pltpu.VMEM(length_line.shape, jnp.int32),
            pltpu.VMEM((leaf_dev * BLK, 2 * HD), f32),
            pltpu.SMEM(matching_lines.shape, jnp.int32),
            pltpu.SemaphoreType.DMA((4,)),
        ],
        vmem=60,
        cost=(leaves * all_cols, 4 * leaves * all_cols, 0),
    )(parts, tail_rows, length_line, picks)
    rows = lax.all_to_all(sends, "node", 0, 0, tiled=True)

    span = GROUP * leaf_dev + 8
    sent = call(
        attend_kernel,
        shape((nodes, span, HD), bf16),
        [HBM] * 6,
        VMEM,
        [
            pltpu.VMEM((extended, rows_all), f32),
            pltpu.VMEM((VROWS, extended), bf16),
            pltpu.VMEM((leaf_dev * BLK, 2 * HD), bf16),
            pltpu.VMEM((block_node.shape[0], rows_all), f32),
            pltpu.VMEM(cache_rows.shape, bf16),
            pltpu.VMEM((nodes, 16, 2 * HD), bf16),
            pltpu.VMEM(ancestry.shape, jnp.int32),
            pltpu.VMEM((1, block_node.shape[0]), jnp.int32),
            pltpu.VMEM((1, leaf_dev), jnp.int32),
            pltpu.SemaphoreType.DMA((5 + key_count // CHUNK,)),
        ],
        vmem=60,
        cost=(4 * rows_all * extended * HD, 8 * HD * key_count, rows_all * extended),
    )(rows, cache_rows, updated, ancestry, block_node.reshape(1, -1), length_line)
    landed = lax.all_to_all(sent, "node", 0, 0, tiled=True)
    mine = call(
        combine_kernel,
        shape(second.shape, bf16),
        [VMEM, VMEM],
        VMEM,
        cost=(10 * rows_all * HD, 4 * rows_all * HD, rows_all * HD),
    )(landed, second)
    attention = lax.all_to_all(mine, "node", 0, 0, tiled=True)
    leaf_out = leaves // heads
    partial_out = call(
        output_kernel,
        shape((leaves, columns), bf16),
        [VMEM, VMEM],
        VMEM,
        cost=(2 * leaves * columns * query_cols, 6 * columns * query_cols, 0),
    )(attention, w_out.T)
    partial_out = lax.all_to_all(
        partial_out.reshape(heads, leaf_out, columns), "head", 0, 0, tiled=True
    )
    projected, squares = call(
        square_kernel,
        (shape((leaf_out, columns), f32), shape((nodes, HD), f32)),
        [VMEM],
        (VMEM, VMEM),
        cost=(leaves * columns, 4 * leaves * columns, 0),
    )(partial_out)
    squares = lax.all_to_all(squares.reshape(nodes, 1, HD), "node", 0, 0, tiled=True)
    children = call(
        children_kernel,
        shape((child_dev, BLK, 2 * HD), bf16),
        [SMEM, VMEM, VMEM],
        VMEM,
        cost=(1000000, 8 * child_dev * BLK * 2 * HD, 0),
    )(matching_lines, rows, attention)
    squares, children = lax.optimization_barrier((squares, children))
    branch = call(
        scale_kernel,
        shape((leaf_out, columns), bf16),
        [VMEM] * 3,
        VMEM,
    )(squares.reshape(nodes, HD), projected, post_gain.reshape(1, columns))
    return (branch, children.reshape(child_dev, BLK, 1, 2 * HD))


def solution(mesh):
    return jax.shard_map(
        shards,
        mesh=mesh,
        in_specs=(
            P(None, "node"),
            P("node", "head"),
            P("node", "head"),
            P("head", "node"),
            P("node"),
            P("node", None, "head", None),
            P("node", None, "head", None),
            P("node"),
            P(),
            P("node"),
            P(),
        ),
        out_specs=(P("head", "node"), P("node", None, "head", None)),
        check_vma=False,
    )
```

time: 145 us -> 140 us (0.966)
  between operations: 14.1 us -> 0.71 us
  blocking collectives: 104 us -> 112 us
  waiting for transfers between devices: 2.21 us -> 6.63 us
  Pallas kernels: 18.4 us -> 16.3 us
    all_to_all x2, blocking collectives: 32.2 us -> 46.7 us  [the longest x1 32.7 us: shards(): rows = lax.all_to_all(sends, 'node', 0, 0, tiled=True)]
    all_to_all x1, blocking collectives: 29.1 us -> 23.8 us  [shards(): lax.all_to_all(partial_out.reshape(heads, leaf_out, columns), 'head', 0,...]
    all_to_all x1, waiting for transfers between devices: 1.53 us -> 6.63 us  [shards(): lax.all_to_all(squares.reshape(nodes, 1, HD), 'node', 0, 0, tiled=True)]
    pallas_call x5, Pallas kernels: 16.8 us -> 14.7 us  [the longest x1 7.6 us: shards(): call(attend_kernel, shape((nodes, span, HD), bf16), [HBM] * 6, VMEM, [plt...]
  transfers between devices with their start and end apart: 2 -> 1, of which waited for: 1 -> 1; matrix products, arithmetic and copies ran while one was open for 1% -> 0% of each run, Pallas kernels for 12% -> 1%
where the time goes in v2:
time: 140 us; the launch traced here: 139 us
  blocking collectives  112 us (80%)
  Pallas kernels  16.3 us (12%)
  waiting for transfers between devices  6.63 us (5%)
  starting transfers between devices  3.8 us (3%)
    all_to_all x1, blocking collectives, shards(): rows = lax.all_to_all(sends, 'node', 0, 0, tiled=True)  32.7 us
    all_to_all x1, blocking collectives, shards(): lax.all_to_all(partial_out.reshape(heads, leaf_out, columns), 'head', 0,...  23.8 us
    all_to_all x1, blocking collectives, shards(): lax.all_to_all(partial.reshape(nodes, leaf_dev, all_cols), 'node', 0, 0,...  23.5 us
    all_to_all x1, blocking collectives, shards(): landed = lax.all_to_all(sent, 'node', 0, 0, tiled=True)  17.8 us
    all_to_all x1, blocking collectives, shards(): attention = lax.all_to_all(mine, 'node', 0, 0, tiled=True)  14 us
    pallas_call x1, Pallas kernels, shards(): call(attend_kernel, shape((nodes, span, HD), bf16), [HBM] * 6, VMEM, [plt...  7.6 us
    all_to_all x1, waiting for transfers between devices, shards(): lax.all_to_all(squares.reshape(nodes, 1, HD), 'node', 0, 0, tiled=True)  6.63 us
    all_to_all x1, starting transfers between devices, shards(): lax.all_to_all(squares.reshape(nodes, 1, HD), 'node', 0, 0, tiled=True)  3.8 us
  transfers between devices with their start and end apart: 1, of which 1 were waited for; matrix products, arithmetic and copies ran while one was open for 0% of the time, Pallas kernels for 1%

profile of v2, /device:TPU:1, one launch (start us, length us, event | category | flops | bytes accessed | tf_op | source)
XLA Modules:
  0.0 139.3 jit_solution(14721787333075982509)
XLA Ops:
  0.6 2.2 %shard_map.122 = (bf16[256,896]{1,0:T(8,128)(2,1)}, s32[8,128]{1,0:T(8,128)}) custom-call(bf16[168,256]{1,0:T(8,128)(2,1)} %bitcast.31, bf16[168,256]{1,0:T(8,128)(2,1)} %query_hbm.1, bf16[168,256]{1,0:T(8,128)(2,1)} %key_value_hbm.1, s32[8,128]{1,0:T(8,128)} %bitcast.21), custom_call_target="tpu_custom_call" | custom-call | flops 77070336 | bytes 1000000 | tf_op jit(solution)/shard_map/pallas_call | solution.py:361
  2.9 23.5 %all_to_all.30 = bf16[32,8,896]{2,1,0:T(8,128)(2,1)} all-to-all(bf16[32,8,896]{2,1,0:T(8,128)(2,1)} %bitcast.26), channel_id=1, replica_groups=mesh['node'=32,'head'=16] {'node'}, dimensions={0} | all-to-all | bytes 917504 | tf_op jit(solution)/shard_map/all_to_all | solution.py:376
  26.4 2.5 %shard_map.123 = (bf16[32,64,256]{2,1,0:T(8,128)(2,1)}, bf16[512,256]{1,0:T(8,128)(2,1)}, bf16[32,16,256]{2,1,0:T(8,128)(2,1)}) custom-call(bf16[256,896]{1,0:T(8,128)(2,1)} %bitcast.24, bf16[512,256]{1,0:T(8,128)(2,1)} %bitcast.27, s32[1,8]{1,0:T(1,128)} %bitcast.28, s32[8,128]{1,0:T(8,128)} %get-tuple-element.12.picks_hbm), custom_call_target="tpu_custom_call" | custom-call | flops 229376 | bytes 917504 | tf_op jit(solution)/shard_map/pallas_call | solution.py:379
  28.9 32.7 %all_to_all.31.rows_hbm.first = bf16[32,64,256]{2,1,0:T(8,128)(2,1)} all-to-all(bf16[32,64,256]{2,1,0:T(8,128)(2,1)} %get-tuple-element.13), channel_id=1, replica_groups=mesh['node'=32,'head'=16] {'node'}, dimensions={0} | all-to-all | bytes 2097152 | tf_op jit(solution)/shard_map/all_to_all | solution.py:399
  61.6 0.0 copy-start.1
  61.6 0.0 copy-start.2
  61.6 0.0 copy-start
  61.6 0.0 copy-start.3
  61.6 7.6 %shard_map.124 = bf16[32,24,128]{2,1,0:T(8,128)(2,1)} custom-call(bf16[32,64,256]{2,1,0:T(8,128)(2,1)} %all_to_all.31.rows_hbm.first, bf16[6144,256]{1,0:T(8,128)(2,1)} %bitcast.30, bf16[512,256]{1,0:T(8,128)(2,1)} %get-tuple-element.14.updated_hbm, s32[256,128]{1,0:T(8,128)} %ancestry_hbm.1, s32[1,96]{1,0:T(1,128)} %bitcast.32, s32[1,8]{1,0:T(1,128)} %bitcast.29), custom_call_target="tpu_custom_call" | custom-call | flops 1744830464 | bytes 6291456 | tf_op jit(solution)/shard_map/pallas_call | solution.py:402
  69.2 0.0 copy-start.4
  69.2 17.8 %all_to_all.32.parts = bf16[32,24,128]{2,1,0:T(8,128)(2,1)S(1)} all-to-all(bf16[32,24,128]{2,1,0:T(8,128)(2,1)} %shard_map.124), channel_id=1, replica_groups=mesh['node'=32,'head'=16] {'node'}, dimensions={0} | all-to-all | bytes 393216 | tf_op jit(solution)/shard_map/all_to_all | solution.py:422
  87.0 0.0 copy-done.1
  87.0 0.4 shard_map.125
  87.4 14.0 %all_to_all.33.attention.second = bf16[32,16,256]{2,1,0:T(8,128)(2,1)S(1)} all-to-all(bf16[32,16,256]{2,1,0:T(8,128)(2,1)S(1)} %shard_map.125), channel_id=1, replica_groups=mesh['node'=32,'head'=16] {'node'}, dimensions={0} | all-to-all | bytes 524288 | tf_op jit(solution)/shard_map/all_to_all | solution.py:430
  101.4 0.0 copy-done.2
  101.4 0.2 shard_map.126
  101.7 23.8 %all_to_all.34.partial = bf16[16,16,168]{2,1,0:T(8,128)(2,1)S(1)} all-to-all(bf16[16,16,168]{2,1,0:T(8,128)(2,1)S(1)} %bitcast.18), channel_id=1, replica_groups=mesh['node'=32,'head'=16] {'head'}, dimensions={0} | all-to-all | bytes 172032 | tf_op jit(solution)/shard_map/all_to_all | solution.py:439
  125.4 0.7 shard_map.127
  126.2 3.8 %all-to-all-start.5 = ((f32[32,1,128]{2,1,0:T(1,128)}), f32[32,1,128]{2,1,0:T(1,128)S(1)}, u32[]{:S(2)}, u32[]{:S(2)}) async-start(f32[32,1,128]{2,1,0:T(1,128)} %bitcast.11), calls=%async_computation.5 | async-start | bytes 32768 | tf_op jit(solution)/shard_map/all_to_all | solution.py:449
  130.0 0.0 copy-done
  130.0 0.0 copy-done.3
  130.0 2.0 %shard_map.128 = bf16[32,64,256]{2,1,0:T(8,128)(2,1)} custom-call(s32[8,128]{1,0:T(8,128)S(1)} %bitcast.22, bf16[32,64,256]{2,1,0:T(8,128)(2,1)S(1)} %copy-done, bf16[32,16,256]{2,1,0:T(8,128)(2,1)S(1)} %all_to_all.33.attention.second), custom_call_target="tpu_custom_call" | custom-call | flops 1000000 | bytes 4194304 | tf_op jit(solution)/shard_map/pallas_call | solution.py:450
  132.0 6.6 %all-to-all-done.5 = f32[32,1,128]{2,1,0:T(1,128)S(1)} async-done(((f32[32,1,128]{2,1,0:T(1,128)}), f32[32,1,128]{2,1,0:T(1,128)S(1)}, u32[]{:S(2)}, u32[]{:S(2)}) %all-to-all-start.5) | async-done | bytes 16416 | tf_op jit(solution)/shard_map/all_to_all | solution.py:449
  138.6 0.0 copy-done.4
  138.6 0.7 shard_map.129
Async XLA Ops:
  61.6 25.4 %copy-start.1 = (bf16[32,16,256]{2,1,0:T(8,128)(2,1)S(1)}, bf16[32,16,256]{2,1,0:T(8,128)(2,1)}, u32[]{:S(2)}) copy-start(bf16[32,16,256]{2,1,0:T(8,128)(2,1)} %get-tuple-element.15.second) | copy-start | bytes 786436
  61.6 39.8 %copy-start.2 = (bf16[256,168]{0,1:T(8,128)(2,1)S(1)}, bf16[256,168]{0,1:T(8,128)(2,1)}, u32[]{:S(2)}) copy-start(bf16[256,168]{0,1:T(8,128)(2,1)} %param.14) | copy-start | bytes 258052
  61.6 68.4 %copy-start = (bf16[32,64,256]{2,1,0:T(8,128)(2,1)S(1)}, bf16[32,64,256]{2,1,0:T(8,128)(2,1)}, u32[]{:S(2)}) copy-start(bf16[32,64,256]{2,1,0:T(8,128)(2,1)} %all_to_all.31.rows_hbm.first) | copy-start | bytes 3145732
  61.6 68.4 %copy-start.3 = (s32[1024]{0:T(1024)S(1)}, s32[1024]{0:T(1024)}, u32[]{:S(2)}) copy-start(s32[1024]{0:T(1024)} %param.21) | copy-start | bytes 12292
  69.2 69.4 %copy-start.4 = (f32[168]{0:T(256)S(1)}, f32[168]{0:T(256)}, u32[]{:S(2)}) copy-start(f32[168]{0:T(256)} %param.15) | copy-start | bytes 2020
  126.2 12.4 %all-to-all-start.5 = ((f32[32,1,128]{2,1,0:T(1,128)}), f32[32,1,128]{2,1,0:T(1,128)S(1)}, u32[]{:S(2)}, u32[]{:S(2)}) async-start(f32[32,1,128]{2,1,0:T(1,128)} %bitcast.11), calls=%async_computation.5 | async-start | bytes 32768 | tf_op jit(solution)/shard_map/all_to_all | solution.py:449

commit v3 on v1

--- a/solution.py
+++ b/solution.py
@@ -1,4 +1,3 @@
-import functools
 import math
 
 import jax
@@ -21,7 +20,7 @@
 epsilon = 1e-06
 f32 = jnp.float32
 bf16 = jnp.bfloat16
-CHUNK = 1024
+CHUNK = 3072
 VROWS = HD + 16
 
 VMEM = pl.BlockSpec(memory_space=pltpu.VMEM)
@@ -51,8 +50,20 @@
     return (rows == cols).astype(f32).astype(bf16)
 
 
-def project_kernel(states_hbm, query_hbm, key_value_hbm, out, states_t, w_query, w_key_value, sems):
-    pairs = ((states_hbm, states_t), (query_hbm, w_query), (key_value_hbm, w_key_value))
+def halves(value):
+    high = value.astype(bf16)
+    return high, (value - high.astype(f32)).astype(bf16)
+
+
+def project_kernel(
+    states_hbm, query_hbm, key_value_hbm, matching_hbm, out, picks, states_t, w_query, w_key_value, matching, sems
+):
+    pairs = (
+        (states_hbm, states_t),
+        (query_hbm, w_query),
+        (key_value_hbm, w_key_value),
+        (matching_hbm, matching),
+    )
     copies = [pltpu.make_async_copy(pair[0], pair[1], sems.at[i]) for i, pair in enumerate(pairs)]
     for copy in copies:
         copy.start()
@@ -60,17 +71,42 @@
     cols = w_query.shape[1]
     copies[0].wait()
     copies[1].wait()
-    out[:, :cols] = lax.dot_general(states_t[...], w_query[...], dims, preferred_element_type=f32)
+    query = lax.dot_general(states_t[...], w_query[...], dims, preferred_element_type=f32)
+    out[:, :cols], out[:, cols : 2 * cols] = halves(query)
     copies[2].wait()
-    out[:, cols:] = lax.dot_general(states_t[...], w_key_value[...], dims, preferred_element_type=f32)
-
-
-def home_kernel(parts, rows_rep, fresh):
-    total = jnp.sum(parts[...], axis=0)
-    pair = jnp.concatenate([total, total], axis=0).astype(bf16)
-    for index in range(rows_rep.shape[0] // 16):
-        rows_rep[pl.ds(index * 16, 16), :] = pair
-    fresh[...] = total[:, total.shape[1] // 2 :]
+    fresh = lax.dot_general(states_t[...], w_key_value[...], dims, preferred_element_type=f32)
+    out[:, 2 * cols :] = fresh.astype(bf16)
+    copies[3].wait()
+    node = lax.axis_index("node")
+    child_dev = matching.shape[0] * HD // lax.axis_size("node")
+    leaf_dev = states_t.shape[1] // lax.axis_size("node")
+    parent = matching[...]
+    first = node * leaf_dev
+    own = (parent >= first) & (parent < first + leaf_dev)
+    part = jnp.where(own, parent - first, 0).astype(f32).astype(bf16)
+    of = lax.broadcasted_iota(jnp.int32, (HD, HD), 0) // child_dev
+    to = lax.broadcasted_iota(jnp.int32, (HD, HD), 1) // child_dev
+    same = (of == to).astype(f32).astype(bf16)
+    picks[...] = jnp.dot(part, same, preferred_element_type=f32).astype(jnp.int32)
+
+
+def home_kernel(parts, query_rep, fresh):
+    leaf_dev = fresh.shape[0]
+    total = jnp.sum(parts[...].astype(f32).reshape(-1, leaf_dev, parts.shape[1]), axis=0)
+    cols = GROUP * HD
+    query = total[:, :cols] + total[:, cols : 2 * cols]
+    pair = jnp.concatenate([query, query], axis=0).astype(bf16)
+    for index in range(query_rep.shape[0] // 16):
+        query_rep[pl.ds(index * 16, 16), :] = pair
+    fresh[...] = total[:, 2 * cols :]
+
+
+def leaf_lengths(lengths):
+    lanes = lax.broadcasted_iota(jnp.int32, lengths.shape, 1)
+    return [
+        jnp.sum(jnp.where(lanes == leaf, lengths[...], 0).astype(f32), axis=1, keepdims=True)
+        for leaf in range(lengths.shape[1])
+    ]
 
 
 def attend_kernel(
@@ -81,6 +117,7 @@
     ancestry_hbm,
     block_node_hbm,
     lengths_hbm,
+    picks_hbm,
     out,
     scores,
     values_t,
@@ -93,9 +130,12 @@
     ancestry,
     block_node,
     lengths,
+    picks,
     sems,
 ):
     node = lax.axis_index("node")
+    nodes = out.shape[0]
+    leaf_dev = lengths.shape[1]
     leaves = queries.shape[0]
     cached = cache.shape[0]
     steps = range(0, cached, CHUNK)
@@ -105,7 +145,8 @@
         (lengths_hbm, lengths),
         (tails_hbm, tails),
         (fresh_hbm, fresh),
-        (rows_hbm.at[:, pl.ds(0, queries.shape[1])], queries),
+        (picks_hbm, picks),
+        (rows_hbm, queries),
     ]
     pairs += [(cache_hbm.at[pl.ds(start, CHUNK), :], cache.at[pl.ds(start, CHUNK), :]) for start in steps]
     copies = [pltpu.make_async_copy(pair[0], pair[1], sems.at[i]) for i, pair in enumerate(pairs)]
@@ -127,14 +168,9 @@
         bias[:, g * leaves : (g + 1) * leaves] = shut
     eye = identity(HD)
     values_t[HD:, :] = jnp.ones((VROWS - HD, values_t.shape[1]), bf16)
-    for copy in copies[2:5]:
+    for copy in copies[2:6]:
         copy.wait()
-    leaf_dev = fresh.shape[0]
-    lanes = lax.broadcasted_iota(jnp.int32, lengths.shape, 1)
-    length = [
-        jnp.sum(jnp.where(lanes == leaf, lengths[...], 0).astype(f32), axis=1, keepdims=True)
-        for leaf in range(leaf_dev)
-    ]
+    length = leaf_lengths(lengths)
     rows = lax.broadcasted_iota(jnp.int32, (BLK, 2 * HD), 0).astype(f32)
     for leaf in range(leaf_dev):
         span = pl.ds(leaf * BLK, BLK)
@@ -143,7 +179,7 @@
         updated[span, :] = block.astype(bf16)
     values_t[:HD, cached:] = matmul_nt(eye, updated[:, HD:]).astype(bf16)
     rows_all = leaves * GROUP
-    copies[5].wait()
+    copies[6].wait()
     query = jnp.concatenate([queries[:, HD * g : HD * (g + 1)] for g in range(GROUP)], axis=0)
     own = updated.shape[0]
     top = jnp.full((8, rows_all), neg_big, f32)
@@ -156,7 +192,7 @@
         scores[pl.ds(cached + leaf * BLK, BLK), :] = part
         top = jnp.maximum(top, jnp.max(part.reshape(BLK // 8, 8, rows_all), axis=0))
     for step, start in enumerate(steps):
-        copies[6 + step].wait()
+        copies[7 + step].wait()
         values_t[:HD, start : start + CHUNK] = matmul_nt(eye, cache[start : start + CHUNK, HD:]).astype(bf16)
         raw = matmul_nt(cache[start : start + CHUNK, :HD], query)
         for block in range(CHUNK // BLK):
@@ -176,32 +212,56 @@
     high = level.astype(bf16).astype(f32)
     middle = (level - high).astype(bf16).astype(f32)
     low = level - high - middle
-    index = lax.broadcasted_iota(jnp.int32, (HD, rows_all), 0)
-    level_t = jnp.where(index == 0, high, jnp.where(index == 1, middle, jnp.where(index == 2, low, 0.0)))
-    for leaf in range(leaf_dev):
-        level_t = jnp.where(index == 3 + leaf, length[leaf], level_t)
-    level_t = level_t.astype(bf16)
+    lines = (nodes * 8, rows_all)
+    line = lax.broadcasted_iota(jnp.int32, lines, 0)
+    row = lax.broadcasted_iota(jnp.int32, lines, 1)
+    part = line % 8
+    level = jnp.where(part == 0, high, jnp.where(part == 1, middle, jnp.where(part == 2, low, 0.0)))
+    level = jnp.where(row % leaves // leaf_dev == line // 8, level, 0.0).astype(bf16)
+    row = lax.broadcasted_iota(jnp.int32, (rows_all, HD), 0)
+    lane = lax.broadcasted_iota(jnp.int32, (rows_all, HD), 1)
+    gather = (row // leaves * leaf_dev + row % leaf_dev == lane).astype(f32).astype(bf16)
+    levels = jnp.dot(level, gather, preferred_element_type=f32)
+    line = lax.broadcasted_iota(jnp.int32, (nodes * 8, picks.shape[0]), 0)
+    spot = lax.broadcasted_iota(jnp.int32, (nodes * 8, picks.shape[0]), 1)
+    per_line = nodes // picks.shape[0]
+    lift = (line // (8 * per_line) == spot).astype(f32).astype(bf16)
+    pick = jnp.dot(lift, picks[...].astype(f32).astype(bf16), preferred_element_type=f32)
+    line = lax.broadcasted_iota(jnp.int32, pick.shape, 0)
+    lane = lax.broadcasted_iota(jnp.int32, pick.shape, 1)
+    chosen = lane == line // 8 % per_line * (HD // per_line)
+    pick = jnp.sum(jnp.where(chosen, pick, 0.0), axis=1, keepdims=True)
+    line = lax.broadcasted_iota(jnp.int32, (nodes * 8, 3 * leaf_dev), 0)
+    of = lax.broadcasted_iota(jnp.int32, (nodes * 8, 3 * leaf_dev), 1)
+    hit = (of % leaf_dev == pick.astype(jnp.int32)) & (of // leaf_dev == line % 8 - 3)
+    sizes = jnp.concatenate([jnp.broadcast_to(value, (1, HD)) for value in length], axis=0)
+    source = jnp.concatenate([sizes, fresh[:, :HD], fresh[:, HD:]], axis=0).astype(bf16)
+    levels = levels + jnp.dot(hit.astype(f32).astype(bf16), source, preferred_element_type=f32)
+    levels = levels.reshape(nodes, 8, HD)
     eye = identity(leaves)
-    nodes = out.shape[0]
-    for part, array in enumerate((mean_t, level_t)):
-        turned = [
-            matmul_nt(eye, array[:, g * leaves : (g + 1) * leaves]).reshape(nodes, leaf_dev, HD)
-            for g in range(GROUP)
-        ]
-        span = GROUP * leaf_dev
-        out[:, part * span : (part + 1) * span, :] = jnp.concatenate(turned, axis=1).astype(bf16)
+    turned = [
+        matmul_nt(eye, mean_t[:, g * leaves : (g + 1) * leaves]).reshape(nodes, leaf_dev, HD)
+        for g in range(GROUP)
+    ]
+    out[...] = jnp.concatenate(turned + [levels], axis=1).astype(bf16)
 
 
 def combine_kernel(parts, out):
-    span = parts.shape[1] // 2
-    mean = parts[:, :span, :].astype(f32)
-    level = parts[:, span:, :].astype(f32)
-    lanes = lax.broadcasted_iota(jnp.int32, level.shape, 2)
-    level = jnp.sum(jnp.where(lanes < 3, level, 0.0), axis=2, keepdims=True)
+    nodes = parts.shape[0]
+    leaf_dev = out.shape[0] // nodes
+    span = GROUP * leaf_dev
+    both = parts[...].astype(f32)
+    mean = both[:, :span, :]
+    lines = both[:, span:, :].reshape(nodes * 8, HD).astype(bf16)
+    row = lax.broadcasted_iota(jnp.int32, (nodes * span, nodes * 8), 0)
+    line = lax.broadcasted_iota(jnp.int32, (nodes * span, nodes * 8), 1)
+    spread = ((row // span == line // 8) & (line % 8 < 3)).astype(f32).astype(bf16)
+    level = jnp.dot(spread, lines, preferred_element_type=f32).reshape(nodes, span, HD)
+    own = lax.broadcasted_iota(jnp.int32, level.shape, 2) == lax.broadcasted_iota(jnp.int32, level.shape, 1)
+    level = jnp.sum(jnp.where(own, level, 0.0), axis=2, keepdims=True)
     top = jnp.max(level, axis=0, keepdims=True)
     weight = jnp.broadcast_to(jnp.exp2(level - top), mean.shape)
     result = jnp.sum(weight * mean, axis=0) / jnp.sum(weight, axis=0)
-    leaf_dev = span // GROUP
     mine = jnp.concatenate([result[g * leaf_dev : (g + 1) * leaf_dev] for g in range(GROUP)], axis=1)
     pair = jnp.concatenate([mine, mine], axis=0).astype(bf16)
     for index in range(out.shape[0] // 16):
@@ -233,26 +293,42 @@
     branch[...] = (projected[...] * inverse * gain[...]).astype(bf16)
 
 
-def children_kernel(leaf_dev, sources, tails, rows_all, levels, out, blocks, fresh, lens, sems):
+def children_kernel(
+    matching_hbm, tails, landed_hbm, out, matching, landed, blocks, built, sems, in_sems, out_sems
+):
+    node = lax.axis_index("node")
     count = out.shape[0]
-    copies = []
+    leaf_dev = tails.shape[0] // landed.shape[0]
+    table = pltpu.make_async_copy(matching_hbm, matching, sems.at[0])
+    table.start()
+    extra = pltpu.make_async_copy(landed_hbm, landed, sems.at[1])
+    extra.start()
+    table.wait()
+    parents = []
+    fetches = []
     for index in range(count):
-        copy = pltpu.make_async_copy(tails.at[sources[index]], blocks.at[index], sems.at[index])
+        place = node * count + index
+        parent = matching[place // HD, place % HD]
+        copy = pltpu.make_async_copy(tails.at[parent], blocks.at[index], in_sems.at[index])
         copy.start()
-        copies.append(copy)
-    span = levels.shape[1] // 2
-    fresh[...] = rows_all[:, rows_all.shape[1] // 2 :].astype(f32)
-    lens[...] = jnp.max(levels[:, span:, :].astype(f32), axis=1)
+        parents.append(parent)
+        fetches.append(copy)
+    extra.wait()
     rows = lax.broadcasted_iota(jnp.int32, (BLK, 2 * HD), 0).astype(f32)
-    lanes = lax.broadcasted_iota(jnp.int32, (1, HD), 1)
+    span = landed.shape[1] - 8
+    stores = []
     for index in range(count):
-        leaf = sources[index]
-        line = lens[pl.ds(leaf // leaf_dev, 1), :]
-        length = jnp.sum(jnp.where(lanes == 3 + leaf % leaf_dev, line, 0.0), axis=1, keepdims=True)
-        copies[index].wait()
+        lines = landed[parents[index] // leaf_dev].astype(f32)[span:]
+        length = lines[3:4, 0:1]
+        fresh = jnp.concatenate([lines[4:5], lines[5:6]], axis=1)
+        fetches[index].wait()
         block = jnp.where(rows < length, blocks[index].astype(f32), 0.0)
-        block = jnp.where(rows == length, fresh[pl.ds(leaf, 1), :], block)
-        out[index] = block.astype(bf16)
+        built[index] = jnp.where(rows == length, fresh, block).astype(bf16)
+        copy = pltpu.make_async_copy(built.at[index], out.at[index], out_sems.at[index])
+        copy.start()
+        stores.append(copy)
+    for copy in stores:
+        copy.wait()
 
 
 def shards(
@@ -270,11 +346,10 @@
 ):
     nodes = lax.axis_size("node")
     heads = lax.axis_size("head")
-    node = lax.axis_index("node")
     leaves = states.shape[0]
     leaf_dev = leaves // nodes
     query_cols = w_query.shape[1]
-    all_cols = query_cols + w_key_value.shape[1]
+    all_cols = 2 * query_cols + w_key_value.shape[1]
     columns = w_out.shape[1]
     rows_all = leaves * GROUP
     child_dev = matching.shape[0] // nodes
@@ -285,37 +360,41 @@
     key_count = cache_rows.shape[0]
     extended = key_count + leaf_dev * BLK
     all_tails = lax.all_gather(tail_rows, "node", axis=0, tiled=True)
-
-    partial = call(
+    matching_lines = matching.reshape(-1, HD)
+    length_line = lengths.reshape(1, -1)
+
+    partial, picks = call(
         project_kernel,
-        shape((leaves, all_cols), f32),
-        [HBM] * 3,
-        VMEM,
+        (shape((leaves, all_cols), bf16), shape(matching_lines.shape, jnp.int32)),
+        [HBM] * 4,
+        (VMEM, VMEM),
         [
             pltpu.VMEM((states.shape[1], leaves), bf16),
             pltpu.VMEM(w_query.shape, bf16),
             pltpu.VMEM(w_key_value.shape, bf16),
-            pltpu.SemaphoreType.DMA((3,)),
+            pltpu.VMEM(matching_lines.shape, jnp.int32),
+            pltpu.SemaphoreType.DMA((4,)),
         ],
         vmem=60,
         cost=(2 * leaves * all_cols * states.shape[1], 1000000, 0),
-    )(states.T, w_query, w_key_value)
+    )(states.T, w_query, w_key_value, matching_lines)
     parts = lax.all_to_all(partial.reshape(nodes, leaf_dev, all_cols), "node", 0, 0, tiled=True)
 
-    rows_rep, fresh = call(
+    parts = parts.reshape(leaves, all_cols)
+    query_rep, fresh = call(
         home_kernel,
-        (shape((leaves, all_cols), bf16), shape((leaf_dev, 2 * HD), f32)),
+        (shape((leaves, query_cols), bf16), shape((leaf_dev, 2 * HD), f32)),
         [VMEM],
         (VMEM, VMEM),
         cost=(leaves * all_cols, 4 * leaves * all_cols, 0),
     )(parts)
-    rows = lax.all_to_all(rows_rep.reshape(nodes, leaf_dev, all_cols), "node", 0, 0, tiled=True)
-    rows = rows.reshape(leaves, all_cols)
-    span = 2 * GROUP * leaf_dev
+    rows = lax.all_to_all(query_rep.reshape(nodes, leaf_dev, query_cols), "node", 0, 0, tiled=True)
+
+    span = GROUP * leaf_dev + 8
     sent = call(
         attend_kernel,
         shape((nodes, span, HD), bf16),
-        [HBM] * 7,
+        [HBM] * 8,
         VMEM,
         [
             pltpu.VMEM((extended, rows_all), f32),
@@ -329,18 +408,20 @@
             pltpu.VMEM(ancestry.shape, jnp.int32),
             pltpu.VMEM((1, block_node.shape[0]), jnp.int32),
             pltpu.VMEM((1, leaf_dev), jnp.int32),
-            pltpu.SemaphoreType.DMA((6 + key_count // CHUNK,)),
+            pltpu.VMEM(picks.shape, jnp.int32),
+            pltpu.SemaphoreType.DMA((7 + key_count // CHUNK,)),
         ],
         vmem=60,
         cost=(4 * rows_all * extended * HD, 8 * HD * key_count, rows_all * extended),
     )(
-        rows,
+        rows.reshape(leaves, query_cols),
         cache_rows,
         tail_rows,
         fresh,
         ancestry,
         block_node.reshape(1, -1),
-        lengths.reshape(1, -1),
+        length_line,
+        picks,
     )
     landed = lax.all_to_all(sent, "node", 0, 0, tiled=True)
     mine = call(
@@ -370,21 +451,23 @@
         cost=(leaves * columns, 4 * leaves * columns, 0),
     )(partial_out)
     squares = lax.all_to_all(squares.reshape(nodes, 1, HD), "node", 0, 0, tiled=True)
-    sources = lax.dynamic_slice_in_dim(matching, node * child_dev, child_dev, 0)
     children = call(
-        functools.partial(children_kernel, leaf_dev),
+        children_kernel,
         shape((child_dev, BLK, 2 * HD), bf16),
-        [SMEM, HBM, VMEM, VMEM],
-        VMEM,
+        [HBM] * 3,
+        HBM,
         [
+            pltpu.SMEM(matching_lines.shape, jnp.int32),
+            pltpu.VMEM(landed.shape, bf16),
             pltpu.VMEM((child_dev, BLK, 2 * HD), bf16),
-            pltpu.VMEM((leaves, 2 * HD), f32),
-            pltpu.VMEM((nodes, HD), f32),
+            pltpu.VMEM((child_dev, BLK, 2 * HD), bf16),
+            pltpu.SemaphoreType.DMA((2,)),
+            pltpu.SemaphoreType.DMA((child_dev,)),
             pltpu.SemaphoreType.DMA((child_dev,)),
         ],
         vmem=60,
-        cost=(1000000, 4 * child_dev * BLK * 2 * HD, 0),
-    )(sources, all_tails.reshape(leaves, BLK, 2 * HD), rows, landed)
+        cost=(1000000, 8 * child_dev * BLK * 2 * HD, 0),
+    )(matching_lines, all_tails.reshape(leaves, BLK, 2 * HD), landed)
     squares, children = lax.optimization_barrier((squares, children))
     branch = call(
         scale_kernel,

time: 145 us -> 134 us (0.924)
  blocking collectives: 104 us -> 91.8 us
  waiting for transfers between devices: 2.21 us -> 7.74 us
  Pallas kernels: 18.4 us -> 16.2 us
    all_gather x1, waiting for transfers between devices: 0.01 us -> 7.06 us  [shards(): all_tails = lax.all_gather(tail_rows, 'node', axis=0, tiled=True)]
    all_to_all x1, blocking collectives: 29.1 us -> 24.4 us  [shards(): lax.all_to_all(partial_out.reshape(heads, leaf_out, columns), 'head', 0,...]
    all_to_all x1, blocking collectives: 18.1 us -> 14.5 us  [shards(): landed = lax.all_to_all(sent, 'node', 0, 0, tiled=True)]
    all_to_all x1, blocking collectives: 24.8 us -> 22.2 us  [shards(): lax.all_to_all(partial.reshape(nodes, leaf_dev, all_cols), 'node', 0, 0,...]
    pallas_call x4, Pallas kernels: 16.5 us -> 14.2 us  [the longest x1 7.78 us: shards(): call(attend_kernel, shape((nodes, span, HD), bf16), [HBM] * 8, VMEM, [plt...]
    all_to_all x1, waiting for transfers between devices: 1.53 us -> 0.01 us  [shards(): lax.all_to_all(squares.reshape(nodes, 1, HD), 'node', 0, 0, tiled=True)]
  transfers between devices with their start and end apart: 2 -> 2, of which waited for: 1 -> 1; matrix products, arithmetic and copies ran while one was open for 1% -> 0% of each run, Pallas kernels for 12% -> 12%
where the time goes in v3:
time: 134 us
  blocking collectives  91.8 us (69%)
  Pallas kernels  16.2 us (12%)
  between operations  14.1 us (11%)
  waiting for transfers between devices  7.74 us (6%)
  starting transfers between devices  3.83 us (3%)
    all_to_all x1, blocking collectives, shards(): lax.all_to_all(partial_out.reshape(heads, leaf_out, columns), 'head', 0,...  24.4 us
    all_to_all x1, blocking collectives, shards(): lax.all_to_all(partial.reshape(nodes, leaf_dev, all_cols), 'node', 0, 0,...  22.2 us
    all_to_all x1, blocking collectives, shards(): lax.all_to_all(query_rep.reshape(nodes, leaf_dev, query_cols), 'node', 0,...  16.8 us
    all_to_all x1, blocking collectives, shards(): landed = lax.all_to_all(sent, 'node', 0, 0, tiled=True)  14.5 us
    all_to_all x1, blocking collectives, shards(): lax.all_to_all(mine.reshape(nodes, leaf_dev, query_cols), 'node', 0, 0, t...  14 us
    pallas_call x1, Pallas kernels, shards(): call(attend_kernel, shape((nodes, span, HD), bf16), [HBM] * 8, VMEM, [plt...  7.78 us
    all_gather x1, waiting for transfers between devices, shards(): all_tails = lax.all_gather(tail_rows, 'node', axis=0, tiled=True)  7.06 us
    pallas_call x1, Pallas kernels, shards(): call(children_kernel, shape((child_dev, BLK, 2 * HD), bf16), [HBM] * 3, H...  4.14 us
  transfers between devices with their start and end apart: 2, of which 1 were waited for; matrix products, arithmetic and copies ran while one was open for 0% of the time, Pallas kernels for 12%

profile of v3, /device:TPU:1, one launch (start us, length us, event | category | flops | bytes accessed | tf_op | source)
XLA Modules:
  0.0 133.7 jit_solution(15136694669943100658)
XLA Ops:
  7.2 0.0 copy-start.1
  7.2 0.0 all-gather.2.cloned.1.call-start
  7.2 0.7 all-gather.2.cloned.1.call-update
  7.9 2.2 %shard_map.122 = (bf16[256,768]{1,0:T(8,128)(2,1)}, s32[8,128]{1,0:T(8,128)}) custom-call(bf16[168,256]{1,0:T(8,128)(2,1)} %bitcast.37, bf16[168,256]{1,0:T(8,128)(2,1)} %query_hbm.1, bf16[168,256]{1,0:T(8,128)(2,1)} %key_value_hbm.1, s32[8,128]{1,0:T(8,128)} %bitcast.38), custom_call_target="tpu_custom_call" | custom-call | flops 66060288 | bytes 1000000 | tf_op jit(solution)/shard_map/pallas_call | solution.py:366
  10.1 22.2 %all_to_all.30 = bf16[32,8,768]{2,1,0:T(8,128)(2,1)S(1)} all-to-all(bf16[32,8,768]{2,1,0:T(8,128)(2,1)} %bitcast.33), channel_id=1, replica_groups=mesh['node'=32,'head'=16] {'node'}, dimensions={0} | all-to-all | bytes 786432 | tf_op jit(solution)/shard_map/all_to_all | solution.py:381
  32.3 0.1 shard_map.123
  32.3 0.0 copy-start.3
  32.4 16.8 %all_to_all.31 = bf16[32,8,256]{2,1,0:T(8,128)(2,1)} all-to-all(bf16[32,8,256]{2,1,0:T(8,128)(2,1)S(1)} %bitcast.27), channel_id=1, replica_groups=mesh['node'=32,'head'=16] {'node'}, dimensions={0} | all-to-all | bytes 262144 | tf_op jit(solution)/shard_map/all_to_all | solution.py:391
  49.2 0.0 copy-done.3
  49.2 0.0 copy-start.2
  49.2 7.8 %shard_map.124 = bf16[32,24,128]{2,1,0:T(8,128)(2,1)} custom-call(bf16[256,256]{1,0:T(8,128)(2,1)} %bitcast.36, bf16[6144,256]{1,0:T(8,128)(2,1)} %bitcast.40, bf16[512,256]{1,0:T(8,128)(2,1)} %bitcast.35, f32[8,256]{1,0:T(8,128)} %copy-done.3, s32[256,128]{1,0:T(8,128)} %ancestry_hbm.1, s32[1,96]{1,0:T(1,128)} %bitcast.41, s32[1,8]{1,0:T(1,128)} %bitcast.42, ...), custom_call_target="tpu_custom_call" | custom-call | flops 1744830464 | bytes 6291456 | tf_op jit(solution)/shard_map/pallas_call | solution.py:394
  57.0 14.5 %all_to_all.32.parts.landed_hbm = bf16[32,24,128]{2,1,0:T(8,128)(2,1)S(1)} all-to-all(bf16[32,24,128]{2,1,0:T(8,128)(2,1)} %shard_map.124), channel_id=1, replica_groups=mesh['node'=32,'head'=16] {'node'}, dimensions={0} | all-to-all | bytes 393216 | tf_op jit(solution)/shard_map/all_to_all | solution.py:426
  71.5 0.0 copy-start
  71.5 0.4 shard_map.125
  71.9 14.0 %all_to_all.33 = bf16[32,8,256]{2,1,0:T(8,128)(2,1)S(1)} all-to-all(bf16[32,8,256]{2,1,0:T(8,128)(2,1)S(1)} %bitcast.26), channel_id=1, replica_groups=mesh['node'=32,'head'=16] {'node'}, dimensions={0} | all-to-all | bytes 262144 | tf_op jit(solution)/shard_map/all_to_all | solution.py:434
  85.9 0.0 copy-done.1
  85.9 0.2 shard_map.126
  86.1 24.4 %all_to_all.34.partial = bf16[16,16,168]{2,1,0:T(8,128)(2,1)S(1)} all-to-all(bf16[16,16,168]{2,1,0:T(8,128)(2,1)S(1)} %bitcast.25), channel_id=1, replica_groups=mesh['node'=32,'head'=16] {'head'}, dimensions={0} | all-to-all | bytes 172032 | tf_op jit(solution)/shard_map/all_to_all | solution.py:443
  110.4 0.7 shard_map.127
  111.1 3.8 %all-to-all-start.5 = ((f32[32,1,128]{2,1,0:T(1,128)}), f32[32,1,128]{2,1,0:T(1,128)S(1)}, u32[]{:S(2)}, u32[]{:S(2)}) async-start(f32[32,1,128]{2,1,0:T(1,128)} %bitcast.15), calls=%async_computation.5 | async-start | bytes 32768 | tf_op jit(solution)/shard_map/all_to_all | solution.py:453
  114.9 7.1 %all-gather.2.cloned.1.call-done = bf16[16384,256]{1,0:T(8,128)(2,1)} async-done(((bf16[512,256]{1,0:T(8,128)(2,1)}), bf16[16384,256]{1,0:T(8,128)(2,1)}) %all-gather.2.cloned.1.call-update) | async-done | bytes 8388624 | tf_op jit(solution)/shard_map/all_gather | solution.py:362
  122.0 0.0 copy-done
  122.0 4.1 %shard_map.128 = bf16[32,64,256]{2,1,0:T(8,128)(2,1)} custom-call(s32[8,128]{1,0:T(8,128)} %bitcast.39, bf16[256,64,256]{2,1,0:T(8,128)(2,1)} %bitcast.31, bf16[32,24,128]{2,1,0:T(8,128)(2,1)} %copy-done), custom_call_target="tpu_custom_call" | custom-call | flops 1000000 | bytes 4194304 | tf_op jit(solution)/shard_map/pallas_call | solution.py:454
  126.1 0.0 all-to-all-done.5
  126.2 0.0 copy-done.2
  126.2 0.7 shard_map.129
Async XLA Ops:
  7.2 78.7 %copy-start.1 = (bf16[256,168]{0,1:T(8,128)(2,1)S(1)}, bf16[256,168]{0,1:T(8,128)(2,1)}, u32[]{:S(2)}) copy-start(bf16[256,168]{0,1:T(8,128)(2,1)} %param.14) | copy-start | bytes 258052
  7.2 114.8 %all-gather.2.cloned.1.call-start = ((), (), s32[]{:S(2)}) async-start(), calls=%async_computation.6 | async-start | bytes 8650752 | tf_op jit(solution)/shard_map/all_gather | solution.py:362
  32.3 16.9 %copy-start.3 = (f32[8,256]{1,0:T(8,128)}, f32[8,256]{1,0:T(8,128)S(1)}, u32[]{:S(2)}) copy-start(f32[8,256]{1,0:T(8,128)S(1)} %get-tuple-element.12.fresh_hbm) | copy-start | bytes 24580
  49.2 77.0 %copy-start.2 = (f32[168]{0:T(256)S(1)}, f32[168]{0:T(256)}, u32[]{:S(2)}) copy-start(f32[168]{0:T(256)} %param.15) | copy-start | bytes 2020
  71.5 50.5 %copy-start = (bf16[32,24,128]{2,1,0:T(8,128)(2,1)}, bf16[32,24,128]{2,1,0:T(8,128)(2,1)S(1)}, u32[]{:S(2)}) copy-start(bf16[32,24,128]{2,1,0:T(8,128)(2,1)S(1)} %all_to_all.32.parts.landed_hbm) | copy-start | bytes 589828
  111.1 15.0 %all-to-all-start.5 = ((f32[32,1,128]{2,1,0:T(1,128)}), f32[32,1,128]{2,1,0:T(1,128)S(1)}, u32[]{:S(2)}, u32[]{:S(2)}) async-start(f32[32,1,128]{2,1,0:T(1,128)} %bitcast.15), calls=%async_computation.5 | async-start | bytes 32768 | tf_op jit(solution)/shard_map/all_to_all | solution.py:453
Sparse Core Ops, SparseCore 0:
  11.2 110.7 all-gather.1

commit v4 on v3

--- a/solution.py
+++ b/solution.py
@@ -22,6 +22,7 @@
 bf16 = jnp.bfloat16
 CHUNK = 3072
 VROWS = HD + 16
+GATHER = 8
 
 VMEM = pl.BlockSpec(memory_space=pltpu.VMEM)
 SMEM = pl.BlockSpec(memory_space=pltpu.SMEM)
@@ -69,14 +70,12 @@
         copy.start()
     dims = (((0,), (0,)), ((), ()))
     cols = w_query.shape[1]
-    copies[0].wait()
-    copies[1].wait()
+    for copy in copies:
+        copy.wait()
     query = lax.dot_general(states_t[...], w_query[...], dims, preferred_element_type=f32)
     out[:, :cols], out[:, cols : 2 * cols] = halves(query)
-    copies[2].wait()
     fresh = lax.dot_general(states_t[...], w_key_value[...], dims, preferred_element_type=f32)
     out[:, 2 * cols :] = fresh.astype(bf16)
-    copies[3].wait()
     node = lax.axis_index("node")
     child_dev = matching.shape[0] * HD // lax.axis_size("node")
     leaf_dev = states_t.shape[1] // lax.axis_size("node")
@@ -316,15 +315,23 @@
     extra.wait()
     rows = lax.broadcasted_iota(jnp.int32, (BLK, 2 * HD), 0).astype(f32)
     span = landed.shape[1] - 8
+    lengths = []
+    fresh = []
+    for parent in parents:
+        lines = landed[parent // leaf_dev].astype(f32)[span:]
+        lengths.append(jnp.broadcast_to(lines[3:4, 0:1], (1, 2 * HD)))
+        fresh.append(jnp.concatenate([lines[4:5], lines[5:6]], axis=1))
     stores = []
-    for index in range(count):
-        lines = landed[parents[index] // leaf_dev].astype(f32)[span:]
-        length = lines[3:4, 0:1]
-        fresh = jnp.concatenate([lines[4:5], lines[5:6]], axis=1)
-        fetches[index].wait()
-        block = jnp.where(rows < length, blocks[index].astype(f32), 0.0)
-        built[index] = jnp.where(rows == length, fresh, block).astype(bf16)
-        copy = pltpu.make_async_copy(built.at[index], out.at[index], out_sems.at[index])
+    for first in range(0, count, GATHER):
+        group = range(first, first + GATHER)
+        for index in group:
+            fetches[index].wait()
+        for index in group:
+            block = jnp.where(rows < lengths[index], blocks[index].astype(f32), 0.0)
+            built[index] = jnp.where(rows == lengths[index], fresh[index], block).astype(bf16)
+        copy = pltpu.make_async_copy(
+            built.at[pl.ds(first, GATHER)], out.at[pl.ds(first, GATHER)], out_sems.at[first // GATHER]
+        )
         copy.start()
         stores.append(copy)
     for copy in stores:
@@ -463,7 +470,7 @@
             pltpu.VMEM((child_dev, BLK, 2 * HD), bf16),
             pltpu.SemaphoreType.DMA((2,)),
             pltpu.SemaphoreType.DMA((child_dev,)),
-            pltpu.SemaphoreType.DMA((child_dev,)),
+            pltpu.SemaphoreType.DMA((child_dev // GATHER,)),
         ],
         vmem=60,
         cost=(1000000, 8 * child_dev * BLK * 2 * HD, 0),

time: 134 us -> 133 us (level)
  transfers between devices with their start and end apart: 2 -> 2, of which waited for: 1 -> 1; matrix products, arithmetic and copies ran while one was open for 0% -> 0% of each run, Pallas kernels for 12% -> 11%
where the time goes in v4:
time: 133 us; the launch traced here: 132 us
  blocking collectives  91.9 us (69%)
  Pallas kernels  15 us (11%)
  between operations  14.1 us (11%)
  waiting for transfers between devices  7.65 us (6%)
  starting transfers between devices  3.83 us (3%)
    all_to_all x1, blocking collectives, shards(): lax.all_to_all(partial_out.reshape(heads, leaf_out, columns), 'head', 0,...  24.3 us
    all_to_all x1, blocking collectives, shards(): lax.all_to_all(partial.reshape(nodes, leaf_dev, all_cols), 'node', 0, 0,...  22.2 us
    all_to_all x1, blocking collectives, shards(): lax.all_to_all(query_rep.reshape(nodes, leaf_dev, query_cols), 'node', 0,...  16.6 us
    all_to_all x1, blocking collectives, shards(): landed = lax.all_to_all(sent, 'node', 0, 0, tiled=True)  14.8 us
    all_to_all x1, blocking collectives, shards(): lax.all_to_all(mine.reshape(nodes, leaf_dev, query_cols), 'node', 0, 0, t...  14 us
    pallas_call x1, Pallas kernels, shards(): call(attend_kernel, shape((nodes, span, HD), bf16), [HBM] * 8, VMEM, [plt...  7.79 us
    all_gather x1, waiting for transfers between devices, shards(): all_tails = lax.all_gather(tail_rows, 'node', axis=0, tiled=True)  6.97 us
    all_to_all x1, starting transfers between devices, shards(): lax.all_to_all(squares.reshape(nodes, 1, HD), 'node', 0, 0, tiled=True)  3.79 us
  transfers between devices with their start and end apart: 2, of which 1 were waited for; matrix products, arithmetic and copies ran while one was open for 0% of the time, Pallas kernels for 11%

profile of v4, /device:TPU:1, one launch (start us, length us, event | category | flops | bytes accessed | tf_op | source)
XLA Modules:
  0.0 132.5 jit_solution(8685729168366445200)
XLA Ops:
  7.2 0.0 copy-start.1
  7.2 0.0 all-gather.2.cloned.1.call-start
  7.2 0.7 all-gather.2.cloned.1.call-update
  7.9 2.0 %shard_map.122 = (bf16[256,768]{1,0:T(8,128)(2,1)}, s32[8,128]{1,0:T(8,128)}) custom-call(bf16[168,256]{1,0:T(8,128)(2,1)} %bitcast.37, bf16[168,256]{1,0:T(8,128)(2,1)} %query_hbm.1, bf16[168,256]{1,0:T(8,128)(2,1)} %key_value_hbm.1, s32[8,128]{1,0:T(8,128)} %bitcast.38), custom_call_target="tpu_custom_call" | custom-call | flops 66060288 | bytes 1000000 | tf_op jit(solution)/shard_map/pallas_call | solution.py:373
  9.9 22.2 %all_to_all.30 = bf16[32,8,768]{2,1,0:T(8,128)(2,1)S(1)} all-to-all(bf16[32,8,768]{2,1,0:T(8,128)(2,1)} %bitcast.33), channel_id=1, replica_groups=mesh['node'=32,'head'=16] {'node'}, dimensions={0} | all-to-all | bytes 786432 | tf_op jit(solution)/shard_map/all_to_all | solution.py:388
  32.1 0.1 shard_map.123
  32.2 0.0 copy-start.3
  32.2 16.6 %all_to_all.31 = bf16[32,8,256]{2,1,0:T(8,128)(2,1)} all-to-all(bf16[32,8,256]{2,1,0:T(8,128)(2,1)S(1)} %bitcast.27), channel_id=1, replica_groups=mesh['node'=32,'head'=16] {'node'}, dimensions={0} | all-to-all | bytes 262144 | tf_op jit(solution)/shard_map/all_to_all | solution.py:398
  48.8 0.0 copy-done.3
  48.8 0.0 copy-start.2
  48.8 7.8 %shard_map.124 = bf16[32,24,128]{2,1,0:T(8,128)(2,1)} custom-call(bf16[256,256]{1,0:T(8,128)(2,1)} %bitcast.36, bf16[6144,256]{1,0:T(8,128)(2,1)} %bitcast.40, bf16[512,256]{1,0:T(8,128)(2,1)} %bitcast.35, f32[8,256]{1,0:T(8,128)} %copy-done.3, s32[256,128]{1,0:T(8,128)} %ancestry_hbm.1, s32[1,96]{1,0:T(1,128)} %bitcast.41, s32[1,8]{1,0:T(1,128)} %bitcast.42, ...), custom_call_target="tpu_custom_call" | custom-call | flops 1744830464 | bytes 6291456 | tf_op jit(solution)/shard_map/pallas_call | solution.py:401
  56.6 14.8 %all_to_all.32.parts.landed_hbm = bf16[32,24,128]{2,1,0:T(8,128)(2,1)S(1)} all-to-all(bf16[32,24,128]{2,1,0:T(8,128)(2,1)} %shard_map.124), channel_id=1, replica_groups=mesh['node'=32,'head'=16] {'node'}, dimensions={0} | all-to-all | bytes 393216 | tf_op jit(solution)/shard_map/all_to_all | solution.py:433
  71.4 0.0 copy-start
  71.4 0.4 shard_map.125
  71.8 14.0 %all_to_all.33 = bf16[32,8,256]{2,1,0:T(8,128)(2,1)S(1)} all-to-all(bf16[32,8,256]{2,1,0:T(8,128)(2,1)S(1)} %bitcast.26), channel_id=1, replica_groups=mesh['node'=32,'head'=16] {'node'}, dimensions={0} | all-to-all | bytes 262144 | tf_op jit(solution)/shard_map/all_to_all | solution.py:441
  85.8 0.0 copy-done.1
  85.8 0.2 shard_map.126
  86.0 24.3 %all_to_all.34.partial = bf16[16,16,168]{2,1,0:T(8,128)(2,1)S(1)} all-to-all(bf16[16,16,168]{2,1,0:T(8,128)(2,1)S(1)} %bitcast.25), channel_id=1, replica_groups=mesh['node'=32,'head'=16] {'head'}, dimensions={0} | all-to-all | bytes 172032 | tf_op jit(solution)/shard_map/all_to_all | solution.py:450
  110.3 0.7 shard_map.127
  111.0 3.8 %all-to-all-start.5 = ((f32[32,1,128]{2,1,0:T(1,128)}), f32[32,1,128]{2,1,0:T(1,128)S(1)}, u32[]{:S(2)}, u32[]{:S(2)}) async-start(f32[32,1,128]{2,1,0:T(1,128)} %bitcast.15), calls=%async_computation.5 | async-start | bytes 32768 | tf_op jit(solution)/shard_map/all_to_all | solution.py:460
  114.8 7.0 %all-gather.2.cloned.1.call-done = bf16[16384,256]{1,0:T(8,128)(2,1)} async-done(((bf16[512,256]{1,0:T(8,128)(2,1)}), bf16[16384,256]{1,0:T(8,128)(2,1)}) %all-gather.2.cloned.1.call-update) | async-done | bytes 8388624 | tf_op jit(solution)/shard_map/all_gather | solution.py:369
  121.8 0.0 copy-done
  121.8 3.1 %shard_map.128 = bf16[32,64,256]{2,1,0:T(8,128)(2,1)} custom-call(s32[8,128]{1,0:T(8,128)} %bitcast.39, bf16[256,64,256]{2,1,0:T(8,128)(2,1)} %bitcast.31, bf16[32,24,128]{2,1,0:T(8,128)(2,1)} %copy-done), custom_call_target="tpu_custom_call" | custom-call | flops 1000000 | bytes 4194304 | tf_op jit(solution)/shard_map/pallas_call | solution.py:461
  124.9 0.0 all-to-all-done.5
  124.9 0.0 copy-done.2
  125.0 0.7 shard_map.129
Async XLA Ops:
  7.2 78.6 %copy-start.1 = (bf16[256,168]{0,1:T(8,128)(2,1)S(1)}, bf16[256,168]{0,1:T(8,128)(2,1)}, u32[]{:S(2)}) copy-start(bf16[256,168]{0,1:T(8,128)(2,1)} %param.14) | copy-start | bytes 258052
  7.2 114.6 %all-gather.2.cloned.1.call-start = ((), (), s32[]{:S(2)}) async-start(), calls=%async_computation.6 | async-start | bytes 8650752 | tf_op jit(solution)/shard_map/all_gather | solution.py:369
  32.2 16.6 %copy-start.3 = (f32[8,256]{1,0:T(8,128)}, f32[8,256]{1,0:T(8,128)S(1)}, u32[]{:S(2)}) copy-start(f32[8,256]{1,0:T(8,128)S(1)} %get-tuple-element.12.fresh_hbm) | copy-start | bytes 24580
  48.8 76.1 %copy-start.2 = (f32[168]{0:T(256)S(1)}, f32[168]{0:T(256)}, u32[]{:S(2)}) copy-start(f32[168]{0:T(256)} %param.15) | copy-start | bytes 2020
  71.4 50.4 %copy-start = (bf16[32,24,128]{2,1,0:T(8,128)(2,1)}, bf16[32,24,128]{2,1,0:T(8,128)(2,1)S(1)}, u32[]{:S(2)}) copy-start(bf16[32,24,128]{2,1,0:T(8,128)(2,1)S(1)} %all_to_all.32.parts.landed_hbm) | copy-start | bytes 589828
  111.0 13.9 %all-to-all-start.5 = ((f32[32,1,128]{2,1,0:T(1,128)}), f32[32,1,128]{2,1,0:T(1,128)S(1)}, u32[]{:S(2)}, u32[]{:S(2)}) async-start(f32[32,1,128]{2,1,0:T(1,128)} %bitcast.15), calls=%async_computation.5 | async-start | bytes 32768 | tf_op jit(solution)/shard_map/all_to_all | solution.py:460
Sparse Core Ops, SparseCore 0:
  11.2 110.5 all-gather.1

commit v5 on v4

--- a/solution.py
+++ b/solution.py
@@ -75,7 +75,8 @@
     query = lax.dot_general(states_t[...], w_query[...], dims, preferred_element_type=f32)
     out[:, :cols], out[:, cols : 2 * cols] = halves(query)
     fresh = lax.dot_general(states_t[...], w_key_value[...], dims, preferred_element_type=f32)
-    out[:, 2 * cols :] = fresh.astype(bf16)
+    key, rest = halves(fresh[:, :HD])
+    out[:, 2 * cols :] = jnp.concatenate([key, rest, fresh[:, HD:].astype(bf16)], axis=1)
     node = lax.axis_index("node")
     child_dev = matching.shape[0] * HD // lax.axis_size("node")
     leaf_dev = states_t.shape[1] // lax.axis_size("node")
@@ -97,7 +98,8 @@
     pair = jnp.concatenate([query, query], axis=0).astype(bf16)
     for index in range(query_rep.shape[0] // 16):
         query_rep[pl.ds(index * 16, 16), :] = pair
-    fresh[...] = total[:, 2 * cols :]
+    total = total[:, 2 * cols :]
+    fresh[...] = jnp.concatenate([total[:, :HD] + total[:, HD : 2 * HD], total[:, 2 * HD :]], axis=1)
 
 
 def leaf_lengths(lengths):
@@ -356,7 +358,7 @@
     leaves = states.shape[0]
     leaf_dev = leaves // nodes
     query_cols = w_query.shape[1]
-    all_cols = 2 * query_cols + w_key_value.shape[1]
+    all_cols = 2 * query_cols + 3 * HD
     columns = w_out.shape[1]
     rows_all = leaves * GROUP
     child_dev = matching.shape[0] // nodes

time: 133 us -> 135 us (1.015)
  blocking collectives: 91.9 us -> 95.3 us
  waiting for transfers between devices: 7.65 us -> 6.17 us
    all_gather x1, waiting for transfers between devices: 6.97 us -> 3.47 us  [shards(): all_tails = lax.all_gather(tail_rows, 'node', axis=0, tiled=True)]
    all_to_all x1, waiting for transfers between devices: 0.01 us -> 2.02 us  [shards(): lax.all_to_all(squares.reshape(nodes, 1, HD), 'node', 0, 0, tiled=True)]
    all_to_all x1, blocking collectives: 24.3 us -> 25.9 us  [shards(): lax.all_to_all(partial_out.reshape(heads, leaf_out, columns), 'head', 0,...]
  transfers between devices with their start and end apart: 2 -> 2, of which waited for: 1 -> 2; matrix products, arithmetic and copies ran while one was open for 0% -> 0% of each run, Pallas kernels for 11% -> 11%
where the time goes in v5:
time: 135 us
  blocking collectives  95.3 us (71%)
  Pallas kernels  15 us (11%)
  between operations  14.1 us (10%)
  waiting for transfers between devices  6.17 us (5%)
  starting transfers between devices  4.05 us (3%)
    all_to_all x1, blocking collectives, shards(): lax.all_to_all(partial_out.reshape(heads, leaf_out, columns), 'head', 0,...  25.9 us
    all_to_all x1, blocking collectives, shards(): lax.all_to_all(partial.reshape(nodes, leaf_dev, all_cols), 'node', 0, 0,...  23.4 us
    all_to_all x1, blocking collectives, shards(): lax.all_to_all(query_rep.reshape(nodes, leaf_dev, query_cols), 'node', 0,...  17.7 us
    all_to_all x1, blocking collectives, shards(): landed = lax.all_to_all(sent, 'node', 0, 0, tiled=True)  14.4 us
    all_to_all x1, blocking collectives, shards(): lax.all_to_all(mine.reshape(nodes, leaf_dev, query_cols), 'node', 0, 0, t...  14 us
    pallas_call x1, Pallas kernels, shards(): call(attend_kernel, shape((nodes, span, HD), bf16), [HBM] * 8, VMEM, [plt...  7.79 us
    all_to_all x1, starting transfers between devices, shards(): lax.all_to_all(squares.reshape(nodes, 1, HD), 'node', 0, 0, tiled=True)  4.01 us
    all_gather x1, waiting for transfers between devices, shards(): all_tails = lax.all_gather(tail_rows, 'node', axis=0, tiled=True)  3.47 us
  transfers between devices with their start and end apart: 2, of which 2 were waited for; matrix products, arithmetic and copies ran while one was open for 0% of the time, Pallas kernels for 11%

profile of v5, /device:TPU:1, one launch (start us, length us, event | category | flops | bytes accessed | tf_op | source)
XLA Modules:
  0.0 134.7 jit_solution(11297077411319876258)
XLA Ops:
  7.2 0.0 copy-start.1
  7.2 0.0 all-gather.2.cloned.1.call-start
  7.2 0.7 all-gather.2.cloned.1.call-update
  7.9 2.1 %shard_map.122 = (bf16[256,896]{1,0:T(8,128)(2,1)}, s32[8,128]{1,0:T(8,128)}) custom-call(bf16[168,256]{1,0:T(8,128)(2,1)} %bitcast.40, bf16[168,256]{1,0:T(8,128)(2,1)} %query_hbm.1, bf16[168,256]{1,0:T(8,128)(2,1)} %key_value_hbm.1, s32[8,128]{1,0:T(8,128)} %bitcast.37), custom_call_target="tpu_custom_call" | custom-call | flops 77070336 | bytes 1000000 | tf_op jit(solution)/shard_map/pallas_call | solution.py:375
  10.0 23.4 %all_to_all.30 = bf16[32,8,896]{2,1,0:T(8,128)(2,1)S(1)} all-to-all(bf16[32,8,896]{2,1,0:T(8,128)(2,1)} %bitcast.33), channel_id=1, replica_groups=mesh['node'=32,'head'=16] {'node'}, dimensions={0} | all-to-all | bytes 917504 | tf_op jit(solution)/shard_map/all_to_all | solution.py:390
  33.4 0.1 shard_map.123
  33.5 0.0 copy-start.3
  33.5 17.7 %all_to_all.31 = bf16[32,8,256]{2,1,0:T(8,128)(2,1)} all-to-all(bf16[32,8,256]{2,1,0:T(8,128)(2,1)S(1)} %bitcast.27), channel_id=1, replica_groups=mesh['node'=32,'head'=16] {'node'}, dimensions={0} | all-to-all | bytes 262144 | tf_op jit(solution)/shard_map/all_to_all | solution.py:400
  51.2 0.0 copy-done.3
  51.2 0.0 copy-start.2
  51.2 7.8 %shard_map.124 = bf16[32,24,128]{2,1,0:T(8,128)(2,1)} custom-call(bf16[256,256]{1,0:T(8,128)(2,1)} %bitcast.36, bf16[6144,256]{1,0:T(8,128)(2,1)} %bitcast.39, bf16[512,256]{1,0:T(8,128)(2,1)} %bitcast.35, f32[8,256]{1,0:T(8,128)} %copy-done.3, s32[256,128]{1,0:T(8,128)} %ancestry_hbm.1, s32[1,96]{1,0:T(1,128)} %bitcast.41, s32[1,8]{1,0:T(1,128)} %bitcast.42, ...), custom_call_target="tpu_custom_call" | custom-call | flops 1744830464 | bytes 6291456 | tf_op jit(solution)/shard_map/pallas_call | solution.py:403
  59.0 14.4 %all_to_all.32.parts.landed_hbm = bf16[32,24,128]{2,1,0:T(8,128)(2,1)S(1)} all-to-all(bf16[32,24,128]{2,1,0:T(8,128)(2,1)} %shard_map.124), channel_id=1, replica_groups=mesh['node'=32,'head'=16] {'node'}, dimensions={0} | all-to-all | bytes 393216 | tf_op jit(solution)/shard_map/all_to_all | solution.py:435
  73.4 0.0 copy-start
  73.4 0.4 shard_map.125
  73.8 14.0 %all_to_all.33 = bf16[32,8,256]{2,1,0:T(8,128)(2,1)S(1)} all-to-all(bf16[32,8,256]{2,1,0:T(8,128)(2,1)S(1)} %bitcast.26), channel_id=1, replica_groups=mesh['node'=32,'head'=16] {'node'}, dimensions={0} | all-to-all | bytes 262144 | tf_op jit(solution)/shard_map/all_to_all | solution.py:443
  87.7 0.0 copy-done.1
  87.7 0.2 shard_map.126
  87.9 25.9 %all_to_all.34.partial = bf16[16,16,168]{2,1,0:T(8,128)(2,1)S(1)} all-to-all(bf16[16,16,168]{2,1,0:T(8,128)(2,1)S(1)} %bitcast.25), channel_id=1, replica_groups=mesh['node'=32,'head'=16] {'head'}, dimensions={0} | all-to-all | bytes 172032 | tf_op jit(solution)/shard_map/all_to_all | solution.py:452
  113.8 0.7 shard_map.127
  114.5 4.0 %all-to-all-start.5 = ((f32[32,1,128]{2,1,0:T(1,128)}), f32[32,1,128]{2,1,0:T(1,128)S(1)}, u32[]{:S(2)}, u32[]{:S(2)}) async-start(f32[32,1,128]{2,1,0:T(1,128)} %bitcast.15), calls=%async_computation.5 | async-start | bytes 32768 | tf_op jit(solution)/shard_map/all_to_all | solution.py:462
  118.5 3.5 %all-gather.2.cloned.1.call-done = bf16[16384,256]{1,0:T(8,128)(2,1)} async-done(((bf16[512,256]{1,0:T(8,128)(2,1)}), bf16[16384,256]{1,0:T(8,128)(2,1)}) %all-gather.2.cloned.1.call-update) | async-done | bytes 8388624 | tf_op jit(solution)/shard_map/all_gather | solution.py:371
  122.0 0.0 copy-done
  122.0 3.1 %shard_map.128 = bf16[32,64,256]{2,1,0:T(8,128)(2,1)} custom-call(s32[8,128]{1,0:T(8,128)} %bitcast.38, bf16[256,64,256]{2,1,0:T(8,128)(2,1)} %bitcast.31, bf16[32,24,128]{2,1,0:T(8,128)(2,1)} %copy-done), custom_call_target="tpu_custom_call" | custom-call | flops 1000000 | bytes 4194304 | tf_op jit(solution)/shard_map/pallas_call | solution.py:463
  125.1 2.0 %all-to-all-done.5 = f32[32,1,128]{2,1,0:T(1,128)S(1)} async-done(((f32[32,1,128]{2,1,0:T(1,128)}), f32[32,1,128]{2,1,0:T(1,128)S(1)}, u32[]{:S(2)}, u32[]{:S(2)}) %all-to-all-start.5) | async-done | bytes 16416 | tf_op jit(solution)/shard_map/all_to_all | solution.py:462
  127.2 0.0 copy-done.2
  127.2 0.7 shard_map.129
Async XLA Ops:
  7.2 80.6 %copy-start.1 = (bf16[256,168]{0,1:T(8,128)(2,1)S(1)}, bf16[256,168]{0,1:T(8,128)(2,1)}, u32[]{:S(2)}) copy-start(bf16[256,168]{0,1:T(8,128)(2,1)} %param.14) | copy-start | bytes 258052
  7.2 114.8 %all-gather.2.cloned.1.call-start = ((), (), s32[]{:S(2)}) async-start(), calls=%async_computation.6 | async-start | bytes 8650752 | tf_op jit(solution)/shard_map/all_gather | solution.py:371
  33.5 17.7 %copy-start.3 = (f32[8,256]{1,0:T(8,128)}, f32[8,256]{1,0:T(8,128)S(1)}, u32[]{:S(2)}) copy-start(f32[8,256]{1,0:T(8,128)S(1)} %get-tuple-element.12.fresh_hbm) | copy-start | bytes 24580
  51.2 76.0 %copy-start.2 = (f32[168]{0:T(256)S(1)}, f32[168]{0:T(256)}, u32[]{:S(2)}) copy-start(f32[168]{0:T(256)} %param.15) | copy-start | bytes 2020
  73.4 48.6 %copy-start = (bf16[32,24,128]{2,1,0:T(8,128)(2,1)}, bf16[32,24,128]{2,1,0:T(8,128)(2,1)S(1)}, u32[]{:S(2)}) copy-start(bf16[32,24,128]{2,1,0:T(8,128)(2,1)S(1)} %all_to_all.32.parts.landed_hbm) | copy-start | bytes 589828
  114.5 12.7 %all-to-all-start.5 = ((f32[32,1,128]{2,1,0:T(1,128)}), f32[32,1,128]{2,1,0:T(1,128)S(1)}, u32[]{:S(2)}, u32[]{:S(2)}) async-start(f32[32,1,128]{2,1,0:T(1,128)} %bitcast.15), calls=%async_computation.5 | async-start | bytes 32768 | tf_op jit(solution)/shard_map/all_to_all | solution.py:462
Sparse Core Ops, SparseCore 0:
  11.2 110.7 all-gather.1

commit v6 on v5

--- a/solution.py
+++ b/solution.py
@@ -57,13 +57,12 @@
 
 
 def project_kernel(
-    states_hbm, query_hbm, key_value_hbm, matching_hbm, out, picks, states_t, w_query, w_key_value, matching, sems
+    states_hbm, query_hbm, key_value_hbm, out, states_t, w_query, w_key_value, sems
 ):
     pairs = (
         (states_hbm, states_t),
         (query_hbm, w_query),
         (key_value_hbm, w_key_value),
-        (matching_hbm, matching),
     )
     copies = [pltpu.make_async_copy(pair[0], pair[1], sems.at[i]) for i, pair in enumerate(pairs)]
     for copy in copies:
@@ -77,17 +76,6 @@
     fresh = lax.dot_general(states_t[...], w_key_value[...], dims, preferred_element_type=f32)
     key, rest = halves(fresh[:, :HD])
     out[:, 2 * cols :] = jnp.concatenate([key, rest, fresh[:, HD:].astype(bf16)], axis=1)
-    node = lax.axis_index("node")
-    child_dev = matching.shape[0] * HD // lax.axis_size("node")
-    leaf_dev = states_t.shape[1] // lax.axis_size("node")
-    parent = matching[...]
-    first = node * leaf_dev
-    own = (parent >= first) & (parent < first + leaf_dev)
-    part = jnp.where(own, parent - first, 0).astype(f32).astype(bf16)
-    of = lax.broadcasted_iota(jnp.int32, (HD, HD), 0) // child_dev
-    to = lax.broadcasted_iota(jnp.int32, (HD, HD), 1) // child_dev
-    same = (of == to).astype(f32).astype(bf16)
-    picks[...] = jnp.dot(part, same, preferred_element_type=f32).astype(jnp.int32)
 
 
 def home_kernel(parts, query_rep, fresh):
@@ -118,7 +106,7 @@
     ancestry_hbm,
     block_node_hbm,
     lengths_hbm,
-    picks_hbm,
+    matching_hbm,
     out,
     scores,
     values_t,
@@ -131,7 +119,7 @@
     ancestry,
     block_node,
     lengths,
-    picks,
+    matching,
     sems,
 ):
     node = lax.axis_index("node")
@@ -146,7 +134,7 @@
         (lengths_hbm, lengths),
         (tails_hbm, tails),
         (fresh_hbm, fresh),
-        (picks_hbm, picks),
+        (matching_hbm, matching),
         (rows_hbm, queries),
     ]
     pairs += [(cache_hbm.at[pl.ds(start, CHUNK), :], cache.at[pl.ds(start, CHUNK), :]) for start in steps]
@@ -172,6 +160,15 @@
     for copy in copies[2:6]:
         copy.wait()
     length = leaf_lengths(lengths)
+    child_dev = matching.shape[0] * HD // nodes
+    parent = matching[...]
+    first = node * leaf_dev
+    mine = (parent >= first) & (parent < first + leaf_dev)
+    part = jnp.where(mine, parent - first, 0).astype(f32).astype(bf16)
+    of = lax.broadcasted_iota(jnp.int32, (HD, HD), 0) // child_dev
+    to = lax.broadcasted_iota(jnp.int32, (HD, HD), 1) // child_dev
+    same = (of == to).astype(f32).astype(bf16)
+    picks = jnp.dot(part, same, preferred_element_type=f32).astype(bf16)
     rows = lax.broadcasted_iota(jnp.int32, (BLK, 2 * HD), 0).astype(f32)
     for leaf in range(leaf_dev):
         span = pl.ds(leaf * BLK, BLK)
@@ -227,7 +224,7 @@
     spot = lax.broadcasted_iota(jnp.int32, (nodes * 8, picks.shape[0]), 1)
     per_line = nodes // picks.shape[0]
     lift = (line // (8 * per_line) == spot).astype(f32).astype(bf16)
-    pick = jnp.dot(lift, picks[...].astype(f32).astype(bf16), preferred_element_type=f32)
+    pick = jnp.dot(lift, picks, preferred_element_type=f32)
     line = lax.broadcasted_iota(jnp.int32, pick.shape, 0)
     lane = lax.broadcasted_iota(jnp.int32, pick.shape, 1)
     chosen = lane == line // 8 % per_line * (HD // per_line)
@@ -372,21 +369,20 @@
     matching_lines = matching.reshape(-1, HD)
     length_line = lengths.reshape(1, -1)
 
-    partial, picks = call(
+    partial = call(
         project_kernel,
-        (shape((leaves, all_cols), bf16), shape(matching_lines.shape, jnp.int32)),
-        [HBM] * 4,
-        (VMEM, VMEM),
+        shape((leaves, all_cols), bf16),
+        [HBM] * 3,
+        VMEM,
         [
             pltpu.VMEM((states.shape[1], leaves), bf16),
             pltpu.VMEM(w_query.shape, bf16),
             pltpu.VMEM(w_key_value.shape, bf16),
-            pltpu.VMEM(matching_lines.shape, jnp.int32),
-            pltpu.SemaphoreType.DMA((4,)),
+            pltpu.SemaphoreType.DMA((3,)),
         ],
         vmem=60,
         cost=(2 * leaves * all_cols * states.shape[1], 1000000, 0),
-    )(states.T, w_query, w_key_value, matching_lines)
+    )(states.T, w_query, w_key_value)
     parts = lax.all_to_all(partial.reshape(nodes, leaf_dev, all_cols), "node", 0, 0, tiled=True)
 
     parts = parts.reshape(leaves, all_cols)
@@ -417,7 +413,7 @@
             pltpu.VMEM(ancestry.shape, jnp.int32),
             pltpu.VMEM((1, block_node.shape[0]), jnp.int32),
             pltpu.VMEM((1, leaf_dev), jnp.int32),
-            pltpu.VMEM(picks.shape, jnp.int32),
+            pltpu.VMEM(matching_lines.shape, jnp.int32),
             pltpu.SemaphoreType.DMA((7 + key_count // CHUNK,)),
         ],
         vmem=60,
@@ -430,7 +426,7 @@
         ancestry,
         block_node.reshape(1, -1),
         length_line,
-        picks,
+        matching_lines,
     )
     landed = lax.all_to_all(sent, "node", 0, 0, tiled=True)
     mine = call(

time: 135 us -> 135 us (level)
  no operation moved by 1% of the time
where the time goes in v6:
time: 135 us
  blocking collectives  95.3 us (71%)
  Pallas kernels  15 us (11%)
  between operations  14.1 us (10%)
  waiting for transfers between devices  6.17 us (5%)
  starting transfers between devices  4.15 us (3%)
    all_to_all x1, blocking collectives, shards(): lax.all_to_all(partial_out.reshape(heads, leaf_out, columns), 'head', 0,...  25.8 us
    all_to_all x1, blocking collectives, shards(): lax.all_to_all(partial.reshape(nodes, leaf_dev, all_cols), 'node', 0, 0,...  23.4 us
    all_to_all x1, blocking collectives, shards(): lax.all_to_all(query_rep.reshape(nodes, leaf_dev, query_cols), 'node', 0,...  17.6 us
    all_to_all x1, blocking collectives, shards(): landed = lax.all_to_all(sent, 'node', 0, 0, tiled=True)  14.5 us
    all_to_all x1, blocking collectives, shards(): lax.all_to_all(mine.reshape(nodes, leaf_dev, query_cols), 'node', 0, 0, t...  14 us
    pallas_call x1, Pallas kernels, shards(): call(attend_kernel, shape((nodes, span, HD), bf16), [HBM] * 8, VMEM, [plt...  7.78 us
    all_to_all x1, starting transfers between devices, shards(): lax.all_to_all(squares.reshape(nodes, 1, HD), 'node', 0, 0, tiled=True)  4.11 us
    all_gather x1, waiting for transfers between devices, shards(): all_tails = lax.all_gather(tail_rows, 'node', axis=0, tiled=True)  3.42 us
  transfers between devices with their start and end apart: 2, of which 2 were waited for; matrix products, arithmetic and copies ran while one was open for 0% of the time, Pallas kernels for 11%

profile of v6, /device:TPU:1, one launch (start us, length us, event | category | flops | bytes accessed | tf_op | source)
XLA Modules:
  0.0 134.7 jit_solution(6554086475480330321)
XLA Ops:
  7.2 0.0 copy-start.1
  7.2 0.0 all-gather.2.cloned.1.call-start
  7.2 0.7 all-gather.2.cloned.1.call-update
  7.9 2.0 %shard_map.122 = bf16[256,896]{1,0:T(8,128)(2,1)} custom-call(bf16[168,256]{1,0:T(8,128)(2,1)} %bitcast.37, bf16[168,256]{1,0:T(8,128)(2,1)} %query_hbm.1, bf16[168,256]{1,0:T(8,128)(2,1)} %key_value_hbm.1), custom_call_target="tpu_custom_call" | custom-call | flops 77070336 | bytes 1000000 | tf_op jit(solution)/shard_map/pallas_call | solution.py:372
  10.0 23.4 %all_to_all.30 = bf16[32,8,896]{2,1,0:T(8,128)(2,1)S(1)} all-to-all(bf16[32,8,896]{2,1,0:T(8,128)(2,1)} %bitcast.32), channel_id=1, replica_groups=mesh['node'=32,'head'=16] {'node'}, dimensions={0} | all-to-all | bytes 917504 | tf_op jit(solution)/shard_map/all_to_all | solution.py:386
  33.4 0.1 shard_map.123
  33.5 0.0 copy-start.3
  33.5 17.6 %all_to_all.31 = bf16[32,8,256]{2,1,0:T(8,128)(2,1)} all-to-all(bf16[32,8,256]{2,1,0:T(8,128)(2,1)S(1)} %bitcast.27), channel_id=1, replica_groups=mesh['node'=32,'head'=16] {'node'}, dimensions={0} | all-to-all | bytes 262144 | tf_op jit(solution)/shard_map/all_to_all | solution.py:396
  51.1 0.0 copy-done.3
  51.1 0.0 copy-start.2
  51.1 7.8 %shard_map.124 = bf16[32,24,128]{2,1,0:T(8,128)(2,1)} custom-call(bf16[256,256]{1,0:T(8,128)(2,1)} %bitcast.36, bf16[6144,256]{1,0:T(8,128)(2,1)} %bitcast.40, bf16[512,256]{1,0:T(8,128)(2,1)} %bitcast.35, f32[8,256]{1,0:T(8,128)} %copy-done.3, s32[256,128]{1,0:T(8,128)} %ancestry_hbm.1, s32[1,96]{1,0:T(1,128)} %bitcast.41, s32[1,8]{1,0:T(1,128)} %bitcast.42, ...), custom_call_target="tpu_custom_call" | custom-call | flops 1744830464 | bytes 6291456 | tf_op jit(solution)/shard_map/pallas_call | solution.py:399
  58.9 14.5 %all_to_all.32.parts.landed_hbm = bf16[32,24,128]{2,1,0:T(8,128)(2,1)S(1)} all-to-all(bf16[32,24,128]{2,1,0:T(8,128)(2,1)} %shard_map.124), channel_id=1, replica_groups=mesh['node'=32,'head'=16] {'node'}, dimensions={0} | all-to-all | bytes 393216 | tf_op jit(solution)/shard_map/all_to_all | solution.py:431
  73.4 0.0 copy-start
  73.4 0.4 shard_map.125
  73.8 14.0 %all_to_all.33 = bf16[32,8,256]{2,1,0:T(8,128)(2,1)S(1)} all-to-all(bf16[32,8,256]{2,1,0:T(8,128)(2,1)S(1)} %bitcast.26), channel_id=1, replica_groups=mesh['node'=32,'head'=16] {'node'}, dimensions={0} | all-to-all | bytes 262144 | tf_op jit(solution)/shard_map/all_to_all | solution.py:439
  87.7 0.0 copy-done.1
  87.8 0.2 shard_map.126
  88.0 25.8 %all_to_all.34.partial = bf16[16,16,168]{2,1,0:T(8,128)(2,1)S(1)} all-to-all(bf16[16,16,168]{2,1,0:T(8,128)(2,1)S(1)} %bitcast.25), channel_id=1, replica_groups=mesh['node'=32,'head'=16] {'head'}, dimensions={0} | all-to-all | bytes 172032 | tf_op jit(solution)/shard_map/all_to_all | solution.py:448
  113.7 0.7 shard_map.127
  114.4 4.1 %all-to-all-start.5 = ((f32[32,1,128]{2,1,0:T(1,128)}), f32[32,1,128]{2,1,0:T(1,128)S(1)}, u32[]{:S(2)}, u32[]{:S(2)}) async-start(f32[32,1,128]{2,1,0:T(1,128)} %bitcast.15), calls=%async_computation.5 | async-start | bytes 32768 | tf_op jit(solution)/shard_map/all_to_all | solution.py:458
  118.6 3.4 %all-gather.2.cloned.1.call-done = bf16[16384,256]{1,0:T(8,128)(2,1)} async-done(((bf16[512,256]{1,0:T(8,128)(2,1)}), bf16[16384,256]{1,0:T(8,128)(2,1)}) %all-gather.2.cloned.1.call-update) | async-done | bytes 8388624 | tf_op jit(solution)/shard_map/all_gather | solution.py:368
  122.0 0.0 copy-done
  122.0 3.1 %shard_map.128 = bf16[32,64,256]{2,1,0:T(8,128)(2,1)} custom-call(s32[8,128]{1,0:T(8,128)} %bitcast.39, bf16[256,64,256]{2,1,0:T(8,128)(2,1)} %bitcast.31, bf16[32,24,128]{2,1,0:T(8,128)(2,1)} %copy-done), custom_call_target="tpu_custom_call" | custom-call | flops 1000000 | bytes 4194304 | tf_op jit(solution)/shard_map/pallas_call | solution.py:459
  125.1 2.1 %all-to-all-done.5 = f32[32,1,128]{2,1,0:T(1,128)S(1)} async-done(((f32[32,1,128]{2,1,0:T(1,128)}), f32[32,1,128]{2,1,0:T(1,128)S(1)}, u32[]{:S(2)}, u32[]{:S(2)}) %all-to-all-start.5) | async-done | bytes 16416 | tf_op jit(solution)/shard_map/all_to_all | solution.py:458
  127.2 0.0 copy-done.2
  127.2 0.7 shard_map.129
Async XLA Ops:
  7.2 80.6 %copy-start.1 = (bf16[256,168]{0,1:T(8,128)(2,1)S(1)}, bf16[256,168]{0,1:T(8,128)(2,1)}, u32[]{:S(2)}) copy-start(bf16[256,168]{0,1:T(8,128)(2,1)} %param.14) | copy-start | bytes 258052
  7.2 114.8 %all-gather.2.cloned.1.call-start = ((), (), s32[]{:S(2)}) async-start(), calls=%async_computation.6 | async-start | bytes 8650752 | tf_op jit(solution)/shard_map/all_gather | solution.py:368
  33.5 17.6 %copy-start.3 = (f32[8,256]{1,0:T(8,128)}, f32[8,256]{1,0:T(8,128)S(1)}, u32[]{:S(2)}) copy-start(f32[8,256]{1,0:T(8,128)S(1)} %get-tuple-element.9.fresh_hbm) | copy-start | bytes 24580
  51.1 76.1 %copy-start.2 = (f32[168]{0:T(256)S(1)}, f32[168]{0:T(256)}, u32[]{:S(2)}) copy-start(f32[168]{0:T(256)} %param.15) | copy-start | bytes 2020
  73.4 48.6 %copy-start = (bf16[32,24,128]{2,1,0:T(8,128)(2,1)}, bf16[32,24,128]{2,1,0:T(8,128)(2,1)S(1)}, u32[]{:S(2)}) copy-start(bf16[32,24,128]{2,1,0:T(8,128)(2,1)S(1)} %all_to_all.32.parts.landed_hbm) | copy-start | bytes 589828
  114.4 12.8 %all-to-all-start.5 = ((f32[32,1,128]{2,1,0:T(1,128)}), f32[32,1,128]{2,1,0:T(1,128)S(1)}, u32[]{:S(2)}, u32[]{:S(2)}) async-start(f32[32,1,128]{2,1,0:T(1,128)} %bitcast.15), calls=%async_computation.5 | async-start | bytes 32768 | tf_op jit(solution)/shard_map/all_to_all | solution.py:458
Sparse Core Ops, SparseCore 0:
  11.2 110.7 all-gather.1
